TPU v7x, 128 devices: a whole 4x4x4 slice. The times are simulated.
128 devices in a mesh: ctx: 32 (over x, z_lo, y), head: 4 (over z_hi, core).
Axes of the slice: x: 4, y: 4, z: 4 (z_hi: 2, z_lo: 2; z = z_hi * 2 + z_lo), core: 2. Of those that a mesh axis runs over, the one named last changes fastest.
Arguments:
- query_states: bfloat16 [512, 8192], P(None, 'ctx'), may hold values from -40 to 40
- key_states: bfloat16 [24576, 8192], P('ctx'), may hold values from -40 to 40
- w_query: bfloat16 [8192, 8192], P('ctx', 'head'), may hold values from -2 to 2
- w_key: bfloat16 [8192, 1024], P(None, 'head'), may hold values from -1 to 1
- w_value: bfloat16 [8192, 1024], P(None, 'head'), may hold values from -0.0625 to 0.0625
- w_out: bfloat16 [8192, 8192], P('head', 'ctx'), may hold values from -2 to 2
- slab_start: int32 [1], replicated, may hold values from 12288 to 24064
Outputs:
- flow_map: float32 [512, 24576], P('head', 'ctx')
All inputs are finite; a program needn't handle non-finite values.
Results may differ from a plain program's by a relative error of at most 0.0033.
The roundings to bfloat16 on the way count: a program that leaves them out, or rounds other values in their place, can miss the bound.
Values may be sent and summed in bfloat16 or wider, within the bound.
No kernel may reach another device: no remote copies, remote signals or barrier semaphores. Data moves between devices by JAX's collectives and lax.ppermute only.
A program may use at most 128 MiB of HBM per device.

v0:
```python
import jax
import jax.numpy as jnp
from jax import lax
from jax.sharding import PartitionSpec as P

HEAD_DIM = 128


masked_value = -1e30


def local(query_states, key_states, w_query, w_key, w_value, w_out, slab_start):
    head_count = lax.axis_size("head")
    query_count = query_states.shape[0]
    key_rows = key_states.shape[0]
    local_heads = w_query.shape[1] // HEAD_DIM
    local_groups = w_key.shape[1] // HEAD_DIM
    group_size = local_heads // local_groups
    partial_queries = jnp.dot(query_states, w_query, preferred_element_type=jnp.float32)
    queries = lax.psum(partial_queries, "ctx").astype(jnp.bfloat16)
    out_blocks = w_out.reshape(local_heads, HEAD_DIM, w_out.shape[1])
    gram_part = jnp.einsum(
        "hae,hbe->hab", out_blocks, out_blocks, preferred_element_type=jnp.float32
    )
    gram_mats = lax.psum(gram_part, "ctx")
    key_proj = (
        jnp.dot(key_states, w_key, preferred_element_type=jnp.float32)
        .astype(jnp.bfloat16)
        .reshape(key_rows, local_groups, HEAD_DIM)
    )
    value_proj = (
        jnp.dot(key_states, w_value, preferred_element_type=jnp.float32)
        .astype(jnp.bfloat16)
        .reshape(key_rows, local_groups, HEAD_DIM)
    )
    value_heads = jnp.repeat(value_proj.astype(jnp.float32), group_size, axis=1)
    projected = jnp.einsum("jha,hab->jhb", value_heads, gram_mats, precision=lax.Precision.HIGHEST)
    value_norm = jnp.sqrt(jnp.sum(projected * value_heads, axis=2) + 1e-06)
    value_norm = value_norm.T.reshape(local_groups, group_size, key_rows)
    query_heads = queries.reshape(query_count, local_groups, group_size, HEAD_DIM)
    scores = jnp.einsum(
        "igxa,jga->gxij", query_heads, key_proj, preferred_element_type=jnp.float32
    ) * HEAD_DIM ** (-0.5)
    slab_first = slab_start[0]
    query_pos = slab_first + jnp.arange(query_count, dtype=jnp.int32)
    key_pos = lax.axis_index("ctx") * key_rows + jnp.arange(key_rows, dtype=jnp.int32)
    visible = key_pos[None, :] <= query_pos[:, None]
    scores = jnp.where(visible, scores, masked_value)
    local_max = jnp.max(scores, axis=3)
    norm_rows = value_norm[:, :, None, :]
    row_max = lax.pmax(local_max.astype(jnp.bfloat16), "ctx").astype(local_max.dtype)
    exp_terms = jnp.where(visible, jnp.exp(scores - row_max[..., None]), 0.0)
    row_sum = lax.psum(jnp.sum(exp_terms, axis=3), "ctx")
    weighted = exp_terms * norm_rows
    contrib_part = jnp.sum(weighted / row_sum[..., None], axis=(0, 1))
    own_count = query_count // head_count
    row_first = lax.axis_index("head") * own_count
    row_pos = (slab_first + row_first + jnp.arange(own_count, dtype=jnp.int32) + 1).astype(
        jnp.float32
    )
    map_rows = lax.psum_scatter(contrib_part, "head", scatter_dimension=0, tiled=True)
    row_total = lax.psum(jnp.sum(map_rows, axis=1), "ctx")
    return row_pos[:, None] * map_rows / row_total[:, None]


def solution(mesh):
    return jax.shard_map(
        local,
        mesh=mesh,
        in_specs=(
            P(None, "ctx"),
            P("ctx", None),
            P("ctx", "head"),
            P(None, "head"),
            P(None, "head"),
            P("head", "ctx"),
            P(),
        ),
        out_specs=P("head", "ctx"),
        check_vma=False,
    )
```

profile of v0, /device:TPU:1, one launch (start us, length us, event | category | flops | bytes accessed | tf_op | source)
XLA Modules:
  0.0 692.1 jit_solution(18084846229653117384)
XLA Ops:
  6.5 0.0 copy-start
  6.5 0.0 all-reduce.3.cloned.1.call-start
  6.5 3.0 fusion.7
  9.6 0.0 all-reduce.3.cloned.1.call-update
  9.6 0.0 reduce-scatter.2.cloned.1.call-start
  10.3 0.0 copy-done
  10.3 3.6 fusion.6
  13.9 170.4 %all-reduce.4 = bf16[512,2048]{1,0:T(8,128)(2,1)} all-reduce(f32[512,2048]{1,0:T(8,128)} %fusion.6), channel_id=1, replica_groups=mesh['ctx'=32,'head'=4] {'ctx'}, use_global_device_ids=true, to_apply=%region_0.0 | all-reduce | flops 1048576 | bytes 6291456 | tf_op jit(solution)/shard_map/psum | solution.py:20
  184.3 2.2 copy.19
  186.5 0.3 broadcast_compare_fusion
  186.8 9.2 %convolution_convert_fusion.1 = bf16[768,256]{0,1:T(8,128)(2,1)S(1)} fusion(bf16[768,8192]{1,0:T(8,128)(2,1)} %param.8, bf16[8192,256]{1,0:T(8,128)(2,1)} %param.10), kind=kOutput, calls=%fused_computation.12 | convolution fusion | flops 3221422080 | bytes 17170432 | tf_op jit(solution)/shard_map/dot_general | solution.py:27
  196.1 10.7 %fusion.1 = (bf16[2,8,512]{2,1,0:T(8,128)(2,1)S(1)}, f32[2,768,512,8]{2,1,3,0:T(8,128)}) fusion(pred[512,768]{0,1:T(8,128)(4,1)S(1)} %broadcast_compare_fusion, bf16[768,2,128,1]{0,2,3,1:T(8,128)(2,1)S(1)} %bitcast.52, bf16[512,2,8,128]{3,2,1,0:T(8,128)(2,1)S(1)} %bitcast.49), kind=kOutput, calls=%fused_computation.4 | convolution fusion | flops 1629478912 | bytes 28065792 | tf_op jit(solution)/shard_map/igxa,jga->gxij/dot_general | solution.py:41
  206.8 131.0 %pmax.7 = bf16[2,8,512]{2,1,0:T(8,128)(2,1)S(1)} all-reduce(bf16[2,8,512]{2,1,0:T(8,128)(2,1)S(1)} %get-tuple-element.5), channel_id=1, replica_groups=mesh['ctx'=32,'head'=4] {'ctx'}, use_global_device_ids=true, to_apply=%region_2.0 | all-reduce | flops 8192 | bytes 32768 | tf_op jit(solution)/shard_map/pmax | solution.py:51
  337.8 11.5 %fusion.2 = f32[2,8,512]{2,1,0:T(8,128)S(1)} fusion(f32[2,768,512,8]{2,1,3,0:T(8,128)} %get-tuple-element.6, f32[2,8,512]{2,1,0:T(8,128)S(1)} %convert_element_type.32, pred[512,768]{0,1:T(8,128)(4,1)S(1)} %broadcast_compare_fusion), kind=kLoop, calls=%fused_computation.5 | loop fusion | flops 31449088 | bytes 25624576 | tf_op jit(solution)/shard_map/reduce_sum | solution.py:53
  349.4 124.6 %psum.30 = f32[2,8,512]{2,1,0:T(8,128)S(1)} all-reduce(f32[2,8,512]{2,1,0:T(8,128)S(1)} %fusion.2), channel_id=1, replica_groups=mesh['ctx'=32,'head'=4] {'ctx'}, use_global_device_ids=true, to_apply=%region_6.7 | all-reduce | flops 8192 | bytes 65536 | tf_op jit(solution)/shard_map/psum | solution.py:53
  473.9 13.8 %bitcast_convert_fusion = f32[768,2,128]{0,2,1:T(8,128)S(1)} fusion(bf16[768,8192]{1,0:T(8,128)(2,1)} %param.8, bf16[8192,256]{1,0:T(8,128)(2,1)} %param.11), kind=kOutput, calls=%fused_computation.19 | convolution fusion | flops 3221618688 | bytes 17563648 | tf_op jit(solution)/shard_map/dot_general | solution.py:32
  487.8 0.0 all-reduce.3.cloned.1.call-done
  487.8 0.6 broadcast_in_dim.24
  488.4 7.1 %fusion.3 = f32[768,16]{0,1:T(8,128)S(1)} fusion(f32[768,2,128]{0,2,1:T(8,128)S(1)} %bitcast_convert_fusion, f32[16,128,128]{1,2,0:T(8,128)} %all-reduce.3.cloned.1.call-done, f32[768,16,128]{0,2,1:T(8,128)S(1)} %bitcast.48), kind=kOutput, calls=%fused_computation.7 | convolution fusion | flops 2419052544 | bytes 8175616 | tf_op jit(solution)/shard_map/jha,hab->jhb/dot_general | solution.py:37
  495.5 0.0 copy-start.1
  495.6 14.0 %fusion = f32[512,768]{0,1:T(8,128)} fusion(f32[2,768,512,8]{2,1,3,0:T(8,128)} %get-tuple-element.6, f32[2,8,512]{2,1,0:T(8,128)S(1)} %psum.30, f32[2,8,768]{2,1,0:T(8,128)S(1)} %sqrt_bitcast_fusion, f32[2,8,512]{2,1,0:T(8,128)S(1)} %convert_element_type.32, pred[512,768]{0,1:T(8,128)(4,1)S(1)} %broadcast_compare_fusion), kind=kLoop, calls=%fused_computation.3 | loop fusion | flops 43646976 | bytes 27246592 | tf_op jit(solution)/shard_map/reduce_sum | solution.py:55
  509.5 0.0 reduce-scatter.2.cloned.1.call-update
  509.6 104.9 %reduce-scatter.2.cloned.1.call-done = f32[128,768]{0,1:T(8,128)} async-done(((f32[512,768]{0,1:T(8,128)}), f32[128,768]{0,1:T(8,128)}) %reduce-scatter.2.cloned.1.call-update) | async-done | bytes 393232 | tf_op jit(solution)/shard_map/reduce_scatter | solution.py:61
  614.5 1.1 reduce_sum.39
  615.6 67.7 %psum.31 = f32[128]{0:T(128)S(1)} all-reduce(f32[128]{0:T(128)S(1)} %reduce_sum.39), channel_id=1, replica_groups=mesh['ctx'=32,'head'=4] {'ctx'}, use_global_device_ids=true, to_apply=%region_10.11 | all-reduce | flops 128 | bytes 1024 | tf_op jit(solution)/shard_map/psum | solution.py:62
  683.3 1.0 multiply_divide_fusion.1
  684.3 0.9 copy.14
  685.2 0.0 copy-done.1
  (5 shorter events, 0.0 us)
Async XLA Ops:
  6.5 3.8 copy-start
  6.5 481.3 %all-reduce.3.cloned.1.call-start = ((), (), s32[]{:S(2)}) async-start(), calls=%async_computation.1 | async-start | bytes 2097152 | tf_op jit(solution)/shard_map/psum | solution.py:25
  9.6 604.9 %reduce-scatter.2.cloned.1.call-start = ((), (), s32[]{:S(2)}) async-start(), calls=%async_computation.2 | async-start | bytes 1966080 | tf_op jit(solution)/shard_map/reduce_scatter | solution.py:61
  495.5 189.7 %copy-start.1 = (bf16[256,2048]{1,0:T(8,128)(2,1)S(1)}, bf16[256,2048]{1,0:T(8,128)(2,1)}, u32[]{:S(2)}) copy-start(bf16[256,2048]{1,0:T(8,128)(2,1)} %param.9) | copy-start | bytes 3145732
Sparse Core Ops, SparseCore 0:
  9.8 291.8 all-reduce.2
  509.7 104.7 reduce-scatter.1
where the time goes:
time: 706 us; the launch traced here: 692 us
  blocking collectives  494 us (70%)
  waiting for transfers between devices  105 us (15%)
  matrix products  47.5 us (7%)
  other arithmetic  28 us (4%)
  between operations  14.2 us (2%)
    psum x1, blocking collectives, local(): queries = lax.psum(partial_queries, 'ctx').astype(jnp.bfloat16)  170 us
    pmax x1, blocking collectives, local(): lax.pmax(local_max.astype(jnp.bfloat16), 'ctx').astype(local_max.dtype)  131 us
    psum x1, blocking collectives, local(): row_sum = lax.psum(jnp.sum(exp_terms, axis=3), 'ctx')  125 us
    reduce_scatter x1, waiting for transfers between devices, local(): lax.psum_scatter(contrib_part, 'head', scatter_dimension=0, tiled=True)  105 us
    psum x1, blocking collectives, local(): row_total = lax.psum(jnp.sum(map_rows, axis=1), 'ctx')  67.7 us
  transfers between devices with their start and end apart: 2, of which 1 were waited for; matrix products, arithmetic and copies ran while one was open for 7% of the time, Pallas kernels for 0%

commit v1 on v0

v1 whole, which is shorter than its diff:
```python
import jax
import jax.numpy as jnp
from jax import lax
from jax.experimental import pallas as pl
from jax.experimental.pallas import tpu as pltpu
from jax.sharding import Mesh, PartitionSpec as P

HEAD_DIM = 128
LOG2E = 1.4426950408889634
MASKED = -1e30
NX, NZ, NY, NH, NC = 4, 2, 4, 2, 2
XZ, CTX, MAP = ("x", "zl"), ("x", "zl", "y"), ("y", "zh", "core")
F32, BF16 = jnp.float32, jnp.bfloat16
VMEM_LIMIT = 56 * 1024 * 1024


def nn(a, b):
    return lax.dot_general(a, b, (((1,), (0,)), ((), ())), preferred_element_type=F32)


def nt(a, b):
    return lax.dot_general(a, b, (((1,), (1,)), ((), ())), preferred_element_type=F32)


def partial_kernel(got_ref, out_ref):
    for c in range(2):
        acc = jnp.zeros((512, 256), F32)
        for s in range(4):
            acc += nn(got_ref[s, 512:1024, :], got_ref[s, c * 256:(c + 1) * 256, :])
        out_ref[:, :, c * 256:(c + 1) * 256] = acc.reshape(8, 64, 256)
    for h in range(4):
        gram = jnp.zeros((128, 128), F32)
        for s in range(4):
            rows = got_ref[s, 1024 + h * 128:1024 + (h + 1) * 128, :]
            gram += nt(rows, rows)
        out_ref[2 * h, :, 512:640] = gram[:64]
        out_ref[2 * h + 1, :, 512:640] = gram[64:]


def scores_kernel(info_ref, q_ref, g_ref, *refs):
    k_refs, v_refs = refs[0:4], refs[4:8]
    p_ref, stat_ref, s_scr, acc_scr = refs[8:12]
    h = pl.program_id(0)
    slab, y, key0 = info_ref[0], info_ref[1], info_ref[2]
    q = q_ref[:, 0].reshape(128, 128)
    gram = jnp.concatenate(
        [g_ref[half, 0, :, b * 128:(b + 1) * 128] for half in range(2) for b in range(4)], axis=0
    )
    row = lax.broadcasted_iota(jnp.int32, (128, 1), 0)
    q_pos = slab + (row // 32) * 128 + y * 32 + row % 32
    lane = lax.broadcasted_iota(jnp.int32, (128, 768), 1)
    peak = jnp.full((128, 1), MASKED, F32)
    for s in range(4):
        first = key0 + ((y + s) % 4) * 768
        scores = nn(q, k_refs[s][...]) * (HEAD_DIM ** -0.5 * LOG2E)
        scores = jnp.where(lane <= q_pos - first, scores, MASKED)
        s_scr[s] = scores
        peak = jnp.maximum(peak, jnp.max(scores, axis=1, keepdims=True))
    e_sum = jnp.zeros((128, 1), F32)
    t_sum = jnp.zeros((128, 1), F32)
    for s in range(4):
        v = v_refs[s][...]
        quad = jnp.sum(nn(gram, v) * v.astype(F32), axis=0, keepdims=True)
        norm = jnp.sqrt(jnp.maximum(quad, 0.0) + 1e-6)
        e = jnp.exp2(s_scr[s] - peak)
        p = e * norm
        e_sum += jnp.sum(e, axis=1, keepdims=True)
        t_sum += jnp.sum(p, axis=1, keepdims=True)
        p_ref[0, s] = p.astype(BF16)
    at = lax.broadcasted_iota(jnp.int32, (128, 128), 1)
    acc = jnp.where(at == h, peak, acc_scr[...])
    acc = jnp.where(at == h + 16, e_sum, acc)
    acc = jnp.where(at == h + 32, t_sum, acc)
    acc_scr[...] = acc

    @pl.when(h == pl.num_programs(0) - 1)
    def _():
        stat_ref[...] = acc.T[:48]


def map_kernel(info_ref, p_ref, own_ref, all_ref, out_ref, w_scr):
    @pl.when(pl.program_id(0) == 0)
    def _():
        peaks = all_ref[:, 0:16, :]
        peak = jnp.max(peaks, axis=0)
        factor = jnp.exp2(peaks - peak[None])
        denom = jnp.sum(all_ref[:, 16:32, :] * factor, axis=0)
        part = jnp.sum(all_ref[:, 32:48, :] * factor, axis=0)
        weight = jnp.exp2(own_ref[0:16, :] - peak) / denom
        total = jnp.sum(part / denom, axis=0, keepdims=True)
        w_scr[...] = jnp.concatenate(
            [weight, total, jnp.zeros((111, 128), F32)], axis=0
        ).T

    acc = jnp.zeros((128, 768), F32)
    for h in range(16):
        acc += p_ref[h, 0].astype(F32) * w_scr[:, h:h + 1]
    out_ref[0, :, 0:768] = acc.astype(BF16)
    total = w_scr[:, 16:17]
    hi = total.astype(BF16).astype(F32)
    lane = lax.broadcasted_iota(jnp.int32, (128, 128), 1)
    out_ref[0, :, 768:896] = jnp.where(
        lane == 0, hi, jnp.where(lane == 1, total - hi, 0.0)
    ).astype(BF16)


def final_kernel(info_ref, got_ref, out_ref):
    slab, head = info_ref[0], info_ref[3]
    for y in range(4):
        rows = got_ref[4 * y].astype(F32)
        for h in range(1, 4):
            rows += got_ref[4 * y + h].astype(F32)
        total = rows[:, 768:769] + rows[:, 769:770]
        row = lax.broadcasted_iota(jnp.int32, (32, 1), 0)
        pos = (slab + head * 128 + y * 32 + row + 1).astype(F32)
        out_ref[y * 32:(y + 1) * 32, :] = rows[:, :768] * (pos / total)


def local(query_states, key_states, w_query, w_key, w_value, w_out, slab_start):
    x, zl, y = lax.axis_index("x"), lax.axis_index("zl"), lax.axis_index("y")
    head = lax.axis_index("zh") * NC + lax.axis_index("core")
    xz = x * NZ + zl
    info = jnp.stack([slab_start[0], y, xz * 3072, head]).astype(jnp.int32)

    rows = query_states.reshape(4, 4, 2, 16, 256).transpose(0, 2, 1, 3, 4).reshape(1, 512, 256)
    columns = w_query.reshape(256, 4, 2, 256).transpose(1, 2, 0, 3).reshape(4, 512, 256)
    pay = jnp.concatenate(
        [columns, jnp.broadcast_to(rows, (4, 512, 256)), w_out.reshape(4, 512, 256)], axis=1
    )
    got = lax.all_to_all(pay, "y", 0, 0, tiled=True)
    parts = pl.pallas_call(
        partial_kernel,
        out_shape=jax.ShapeDtypeStruct((8, 64, 640), F32),
        in_specs=[pl.BlockSpec(memory_space=pltpu.VMEM)],
        out_specs=pl.BlockSpec(memory_space=pltpu.VMEM),
        compiler_params=pltpu.CompilerParams(vmem_limit_bytes=VMEM_LIMIT),
        name="partial",
    )(got)
    parts = lax.all_to_all(parts, XZ, 0, 0, tiled=True)
    summed = jnp.sum(parts, axis=0).astype(BF16)
    queries = summed[:, :512].reshape(4, 16, 512)
    gram = summed[:, 512:].reshape(4, 16, 128).transpose(1, 0, 2).reshape(1, 16, 512)
    block = jnp.concatenate([queries, jnp.broadcast_to(gram, (4, 16, 512))], axis=1)
    block = jnp.broadcast_to(block[None], (8, 4, 32, 512)).reshape(32, 32, 512)
    block = lax.all_to_all(block, CTX, 0, 0, tiled=True).reshape(8, 4, 32, 512)

    w_kv = jnp.concatenate([w_key, w_value], axis=1)
    own_kv = lax.dot_general(
        w_kv, key_states, (((0,), (1,)), ((), ())), preferred_element_type=F32
    ).astype(BF16)
    kv = [own_kv] + [
        lax.ppermute(own_kv, "y", [(i, (i - s) % NY) for i in range(NY)]) for s in (1, 2, 3)
    ]

    p, stats = pl.pallas_call(
        scores_kernel,
        out_shape=(
            jax.ShapeDtypeStruct((16, 4, 128, 768), BF16),
            jax.ShapeDtypeStruct((48, 128), F32),
        ),
        grid_spec=pltpu.PrefetchScalarGridSpec(
            num_scalar_prefetch=1,
            grid=(16,),
            in_specs=[
                pl.BlockSpec((8, 1, 16, 128), lambda h, i: (0, h // 4, 0, h % 4)),
                pl.BlockSpec((2, 1, 16, 512), lambda h, i: (h % 4, h // 4, 1, 0)),
            ]
            + [pl.BlockSpec((128, 768), lambda h, i: (h // 8, 0))] * 4
            + [pl.BlockSpec((128, 768), lambda h, i: (2 + h // 8, 0))] * 4,
            out_specs=(
                pl.BlockSpec((1, 4, 128, 768), lambda h, i: (h, 0, 0, 0)),
                pl.BlockSpec((48, 128), lambda h, i: (0, 0)),
            ),
            scratch_shapes=[pltpu.VMEM((4, 128, 768), F32), pltpu.VMEM((128, 128), F32)],
        ),
        compiler_params=pltpu.CompilerParams(vmem_limit_bytes=VMEM_LIMIT),
        name="scores",
    )(info, block, block, *kv, *kv)

    all_stats = lax.all_to_all(
        jnp.broadcast_to(stats[None], (8, 48, 128)), XZ, 0, 0, tiled=True
    )

    pay = pl.pallas_call(
        map_kernel,
        out_shape=jax.ShapeDtypeStruct((4, 128, 896), BF16),
        grid_spec=pltpu.PrefetchScalarGridSpec(
            num_scalar_prefetch=1,
            grid=(4,),
            in_specs=[
                pl.BlockSpec((16, 1, 128, 768), lambda s, i: (0, s, 0, 0)),
                pl.BlockSpec((48, 128), lambda s, i: (0, 0)),
                pl.BlockSpec((8, 48, 128), lambda s, i: (0, 0, 0)),
            ],
            out_specs=pl.BlockSpec((1, 128, 896), lambda s, i: ((i[1] + s) % 4, 0, 0)),
            scratch_shapes=[pltpu.VMEM((128, 128), F32)],
        ),
        compiler_params=pltpu.CompilerParams(vmem_limit_bytes=VMEM_LIMIT),
        name="weigh",
    )(info, p, stats, all_stats)
    got = lax.all_to_all(pay.reshape(16, 32, 896), MAP, 0, 0, tiled=True)

    return pl.pallas_call(
        final_kernel,
        out_shape=jax.ShapeDtypeStruct((128, 768), F32),
        in_specs=[
            pl.BlockSpec(memory_space=pltpu.SMEM),
            pl.BlockSpec(memory_space=pltpu.VMEM),
        ],
        out_specs=pl.BlockSpec(memory_space=pltpu.VMEM),
        compiler_params=pltpu.CompilerParams(vmem_limit_bytes=VMEM_LIMIT),
        name="finish",
    )(info, got)


def solution(mesh):
    fine = Mesh(
        mesh.devices.reshape(NX, NZ, NY, NH, NC), ("x", "zl", "y", "zh", "core")
    )
    head = ("zh", "core")
    return jax.shard_map(
        local,
        mesh=fine,
        in_specs=(
            P(None, CTX),
            P(CTX, None),
            P(CTX, head),
            P(None, head),
            P(None, head),
            P(head, CTX),
            P(),
        ),
        out_specs=P(head, CTX),
        check_vma=False,
    )
```

time: 706 us -> 197 us (0.28); the launches traced: 692 us -> 196 us
  blocking collectives: 494 us -> 99.1 us
  waiting for transfers between devices: 105 us -> 31.1 us
  Pallas kernels: 0 us -> 35.8 us
  matrix products: 47.5 us -> 13.8 us
  other arithmetic: 28 us -> 0.89 us
  between operations: 14.2 us -> 0.8 us
  starting transfers between devices: 0.04 us -> 8.98 us
    psum x3 -> x0, blocking collectives: 363 us -> none  [the longest x1 170 us: local(): queries = lax.psum(partial_queries, 'ctx').astype(jnp.bfloat16)]
    pmax x1 -> x0, blocking collectives: 131 us -> none  [local(): lax.pmax(local_max.astype(jnp.bfloat16), 'ctx').astype(local_max.dtype)]
    reduce_scatter x1 -> x0, waiting for transfers between devices: 105 us -> none  [local(): lax.psum_scatter(contrib_part, 'head', scatter_dimension=0, tiled=True)]
    all_to_all x0 -> x4, blocking collectives: none -> 99.1 us  [the longest x1 41.6 us: local(): got = lax.all_to_all(pay, 'y', 0, 0, tiled=True)]
    pallas_call x0 -> x4, Pallas kernels: none -> 35.8 us  [the longest x1 21.8 us: local(): pl.pallas_call(scores_kernel, out_shape=(jax.ShapeDtypeStruct((16, 4, 128...]
    dot_general x6 -> x1, matrix products: 47.5 us -> 13.8 us  [local(): lax.dot_general(w_kv, key_states, (((0,), (1,)), ((), ())), preferred_ele...]
    ppermute x0 -> x3, waiting for transfers between devices: none -> 31.1 us  [local(): lax.ppermute(own_kv, 'y', [(i, (i - s) % NY) for i in range(NY)])]
    reduce_sum x3 -> x1, other arithmetic: 26.6 us -> 0.06 us  [local(): summed = jnp.sum(parts, axis=0).astype(BF16)]
  transfers between devices with their start and end apart: 2 -> 4, of which waited for: 1 -> 3; matrix products, arithmetic and copies ran while one was open for 7% -> 7% of each run, Pallas kernels for 0% -> 0%
where the time goes in v1:
time: 197 us; the launch traced here: 196 us
  blocking collectives  99.1 us (50%)
  Pallas kernels  35.8 us (18%)
  waiting for transfers between devices  31.1 us (16%)
  matrix products  13.8 us (7%)
  starting transfers between devices  8.98 us (5%)
  local copies, waits for them, and re-layouts  6.05 us (3%)
    all_to_all x1, blocking collectives, local(): got = lax.all_to_all(pay, 'y', 0, 0, tiled=True)  41.6 us
    ppermute x3, waiting for transfers between devices, local(): lax.ppermute(own_kv, 'y', [(i, (i - s) % NY) for i in range(NY)])  31.1 us
    all_to_all x1, blocking collectives, local(): got = lax.all_to_all(pay.reshape(16, 32, 896), MAP, 0, 0, tiled=True)  26.2 us
    pallas_call x1, Pallas kernels, local(): pl.pallas_call(scores_kernel, out_shape=(jax.ShapeDtypeStruct((16, 4, 128...  21.8 us
    all_to_all x1, blocking collectives, local(): parts = lax.all_to_all(parts, XZ, 0, 0, tiled=True)  21 us
    dot_general x1, matrix products, local(): lax.dot_general(w_kv, key_states, (((0,), (1,)), ((), ())), preferred_ele...  13.8 us
    all_to_all x1, blocking collectives, local(): lax.all_to_all(jnp.broadcast_to(stats[None], (8, 48, 128)), XZ, 0, 0, til...  10.4 us
    pallas_call x1, Pallas kernels, local(): pl.pallas_call(map_kernel, out_shape=jax.ShapeDtypeStruct((4, 128, 896),...  7.99 us
  transfers between devices with their start and end apart: 4, of which 3 were waited for; matrix products, arithmetic and copies ran while one was open for 7% of the time, Pallas kernels for 0%

profile of v1, /device:TPU:1, one launch (start us, length us, event | category | flops | bytes accessed | tf_op | source)
XLA Modules:
  0.0 196.5 jit_solution(14252188408197405756)
XLA Ops:
  0.0 1.1 copy.9
  1.1 1.8 reshape.33
  2.9 0.2 copy.8
  3.1 0.1 broadcast_in_dim.13
  3.2 0.0 copy-done.4
  3.2 0.3 pad_maximum_fusion
  3.5 41.6 %all_to_all.25.got_ref = bf16[4,1536,256]{2,1,0:T(8,128)(2,1)} all-to-all(bf16[4,1536,256]{2,1,0:T(8,128)(2,1)S(1)} %pad_maximum_fusion), channel_id=1, replica_groups=mesh['x'=4,'zl'=2,'y'=4,'zh'=2,'core'=2] {'y'}, dimensions={0} | all-to-all | bytes 6291456 | tf_op jit(solution)/shard_map/all_to_all | solution.py:130
  45.0 3.9 %partial.1 = f32[8,64,640]{2,1,0:T(8,128)} custom-call(bf16[4,1536,256]{2,1,0:T(8,128)(2,1)} %all_to_all.25.got_ref), custom_call_target="tpu_custom_call" | custom-call | tf_op jit(solution)/shard_map/partial/pallas_call | solution.py:131
  49.0 21.0 %all_to_all.26 = f32[8,64,640]{2,1,0:T(8,128)S(1)} all-to-all(f32[8,64,640]{2,1,0:T(8,128)} %partial.1), channel_id=1, replica_groups=mesh['x'=4,'zl'=2,'y'=4,'zh'=2,'core'=2] {'x','zl'}, dimensions={0} | all-to-all | bytes 2621440 | tf_op jit(solution)/shard_map/all_to_all | solution.py:139
  70.0 0.1 reduce_sum.9
  70.2 1.1 broadcast_in_dim.30
  71.2 4.1 %all-to-all-start.2 = ((bf16[32,32,512]{2,1,0:T(8,128)(2,1)}), bf16[32,32,512]{2,1,0:T(8,128)(2,1)S(1)}, u32[]{:S(2)}, u32[]{:S(2)}) async-start(bf16[32,32,512]{2,1,0:T(8,128)(2,1)} %bitcast.12), calls=%async_computation.2 | async-start | bytes 2097152 | tf_op jit(solution)/shard_map/all_to_all | solution.py:145
  75.4 13.8 %fusion.4.refs_0_.refs_4_ = bf16[512,768]{1,0:T(8,128)(2,1)S(1)} fusion(bf16[768,8192]{1,0:T(8,128)(2,1)} %param.8, bf16[8192,256]{1,0:T(8,128)(2,1)} %param.11, bf16[8192,256]{1,0:T(8,128)(2,1)} %param.10), kind=kOutput, calls=%fused_computation.5 | convolution fusion | flops 6459621376 | bytes 21757952 | tf_op jit(solution)/shard_map/dot_general | solution.py:148
  89.1 0.0 copy-start.1
  89.1 1.3 collective-permute-start.2
  90.4 2.4 %collective-permute-start.1 = (bf16[512,768]{1,0:T(8,128)(2,1)S(1)}, bf16[512,768]{1,0:T(8,128)(2,1)S(1)}, u32[]{:S(2)}, u32[]{:S(2)}) collective-permute-start(bf16[512,768]{1,0:T(8,128)(2,1)S(1)} %fusion.4.refs_0_.refs_4_), channel_id=1, source_target_pairs={{0,8},{4,12},{8,0},{12,4},{1,9},{5,13},{9,1},{13,5},{2,10},{6,14},... | collective-permute-start | bytes 2359304 | tf_op jit(solution)/shard_map/ppermute | solution.py:152
  92.8 1.2 collective-permute-start
  94.7 0.6 pad_add_fusion.info_ref
  95.2 10.7 %collective-permute-done.2.refs_3_.refs_7_ = bf16[512,768]{1,0:T(8,128)(2,1)S(1)} collective-permute-done((bf16[512,768]{1,0:T(8,128)(2,1)S(1)}, bf16[512,768]{1,0:T(8,128)(2,1)S(1)}, u32[]{:S(2)}, u32[]{:S(2)}) %collective-permute-start.2) | collective-permute-done | bytes 786464 | tf_op jit(solution)/shard_map/ppermute | solution.py:152
  105.9 17.5 %collective-permute-done.1.refs_2_.refs_6_ = bf16[512,768]{1,0:T(8,128)(2,1)S(1)} collective-permute-done((bf16[512,768]{1,0:T(8,128)(2,1)S(1)}, bf16[512,768]{1,0:T(8,128)(2,1)S(1)}, u32[]{:S(2)}, u32[]{:S(2)}) %collective-permute-start.1) | collective-permute-done | bytes 786464 | tf_op jit(solution)/shard_map/ppermute | solution.py:152
  123.4 2.8 %collective-permute-done.refs_1_.refs_5_ = bf16[512,768]{1,0:T(8,128)(2,1)} collective-permute-done((bf16[512,768]{1,0:T(8,128)(2,1)S(1)}, bf16[512,768]{1,0:T(8,128)(2,1)}, u32[]{:S(2)}, u32[]{:S(2)}) %collective-permute-start) | collective-permute-done | bytes 786464 | tf_op jit(solution)/shard_map/ppermute | solution.py:152
  126.3 0.0 all-to-all-done.2
  126.3 0.0 copy-done.1
  126.3 0.0 copy-done.2
  126.3 0.0 copy-done.3
  126.3 1.0 copy-done
  127.3 21.8 %scores.1 = (bf16[16,4,128,768]{3,2,1,0:T(8,128)(2,1)}, f32[48,128]{1,0:T(8,128)}) custom-call(s32[4]{0:T(128)} %pad_add_fusion.info_ref, bf16[8,4,32,512]{3,2,1,0:T(8,128)(2,1)} %bitcast.22, bf16[8,4,32,512]{3,2,1,0:T(8,128)(2,1)} %bitcast.23, bf16[512,768]{1,0:T(8,128)(2,1)} %copy-done.1, bf16[512,768]{1,0:T(8,128)(2,1)} %collective-permute-done.refs_1_.refs_5_, ...), custom_call_target="tpu_custom_call" | custom-call | tf_op jit(solution)/shard_map/scores/pallas_call | solution.py:155
  149.1 0.8 broadcast_in_dim.31
  149.8 10.4 %all_to_all.27.all_ref = f32[8,48,128]{2,1,0:T(8,128)} all-to-all(f32[8,48,128]{2,1,0:T(8,128)S(1)} %broadcast_in_dim.31), channel_id=1, replica_groups=mesh['x'=4,'zl'=2,'y'=4,'zh'=2,'core'=2] {'x','zl'}, dimensions={0} | all-to-all | bytes 393216 | tf_op jit(solution)/shard_map/all_to_all | solution.py:180
  160.2 8.0 %weigh.1 = bf16[4,128,896]{2,1,0:T(8,128)(2,1)} custom-call(s32[4]{0:T(128)} %pad_add_fusion.info_ref, bf16[16,4,128,768]{3,2,1,0:T(8,128)(2,1)} %get-tuple-element.7.p_ref, f32[48,128]{1,0:T(8,128)} %get-tuple-element.8.own_ref, f32[8,48,128]{2,1,0:T(8,128)} %all_to_all.27.all_ref), custom_call_target="tpu_custom_call" | custom-call | tf_op jit(solution)/shard_map/weigh/pallas_call | solution.py:184
  168.2 26.2 %all_to_all.28.got_ref = bf16[16,32,896]{2,1,0:T(8,128)(2,1)} all-to-all(bf16[16,32,896]{2,1,0:T(8,128)(2,1)} %bitcast.25), channel_id=1, replica_groups=mesh['x'=4,'zl'=2,'y'=4,'zh'=2,'core'=2] {'y','zh','core'}, dimensions={0} | all-to-all | bytes 1835008 | tf_op jit(solution)/shard_map/all_to_all | solution.py:201
  194.4 2.1 %finish.1 = f32[128,768]{1,0:T(8,128)} custom-call(s32[4]{0:T(128)} %pad_add_fusion.info_ref, bf16[16,32,896]{2,1,0:T(8,128)(2,1)} %all_to_all.28.got_ref), custom_call_target="tpu_custom_call" | custom-call | tf_op jit(solution)/shard_map/finish/pallas_call | solution.py:203
  (10 shorter events, 0.0 us)
Async XLA Ops:
  0.0 3.2 %copy-start.4 = (bf16[2048,256]{1,0:T(8,128)(2,1)S(1)}, bf16[2048,256]{1,0:T(8,128)(2,1)}, u32[]{:S(2)}) copy-start(bf16[2048,256]{1,0:T(8,128)(2,1)} %param.12) | copy-start | bytes 3145732
  71.2 55.0 %all-to-all-start.2 = ((bf16[32,32,512]{2,1,0:T(8,128)(2,1)}), bf16[32,32,512]{2,1,0:T(8,128)(2,1)S(1)}, u32[]{:S(2)}, u32[]{:S(2)}) async-start(bf16[32,32,512]{2,1,0:T(8,128)(2,1)} %bitcast.12), calls=%async_computation.2 | async-start | bytes 2097152 | tf_op jit(solution)/shard_map/all_to_all | solution.py:145
  89.1 37.2 %copy-start.1 = (bf16[512,768]{1,0:T(8,128)(2,1)}, bf16[512,768]{1,0:T(8,128)(2,1)S(1)}, u32[]{:S(2)}) copy-start(bf16[512,768]{1,0:T(8,128)(2,1)S(1)} %fusion.4.refs_0_.refs_4_) | copy-start | bytes 2359300
  89.1 16.8 %collective-permute-start.2 = (bf16[512,768]{1,0:T(8,128)(2,1)S(1)}, bf16[512,768]{1,0:T(8,128)(2,1)S(1)}, u32[]{:S(2)}, u32[]{:S(2)}) collective-permute-start(bf16[512,768]{1,0:T(8,128)(2,1)S(1)} %fusion.4.refs_0_.refs_4_), channel_id=1, source_target_pairs={{0,4},{4,8},{8,12},{12,0},{1,5},{5,9},{9,13},{13,1},{2,6},{6,10},{... | collective-permute-start | bytes 2359304 | tf_op jit(solution)/shard_map/ppermute | solution.py:152
  90.4 33.0 %collective-permute-start.1 = (bf16[512,768]{1,0:T(8,128)(2,1)S(1)}, bf16[512,768]{1,0:T(8,128)(2,1)S(1)}, u32[]{:S(2)}, u32[]{:S(2)}) collective-permute-start(bf16[512,768]{1,0:T(8,128)(2,1)S(1)} %fusion.4.refs_0_.refs_4_), channel_id=1, source_target_pairs={{0,8},{4,12},{8,0},{12,4},{1,9},{5,13},{9,1},{13,5},{2,10},{6,14},... | collective-permute-start | bytes 2359304 | tf_op jit(solution)/shard_map/ppermute | solution.py:152
  92.8 33.5 %collective-permute-start = (bf16[512,768]{1,0:T(8,128)(2,1)S(1)}, bf16[512,768]{1,0:T(8,128)(2,1)}, u32[]{:S(2)}, u32[]{:S(2)}) collective-permute-start(bf16[512,768]{1,0:T(8,128)(2,1)S(1)} %fusion.4.refs_0_.refs_4_), channel_id=1, source_target_pairs={{0,12},{4,0},{8,4},{12,8},{1,13},{5,1},{9,5},{13,9},{2,14},{6,2},{... | collective-permute-start | bytes 2359304 | tf_op jit(solution)/shard_map/ppermute | solution.py:152
  105.9 20.4 %copy-start.2 = (bf16[512,768]{1,0:T(8,128)(2,1)}, bf16[512,768]{1,0:T(8,128)(2,1)S(1)}, u32[]{:S(2)}) copy-start(bf16[512,768]{1,0:T(8,128)(2,1)S(1)} %collective-permute-done.2.refs_3_.refs_7_) | copy-start | bytes 2359300
  123.4 2.9 %copy-start.3 = (bf16[512,768]{1,0:T(8,128)(2,1)}, bf16[512,768]{1,0:T(8,128)(2,1)S(1)}, u32[]{:S(2)}) copy-start(bf16[512,768]{1,0:T(8,128)(2,1)S(1)} %collective-permute-done.1.refs_2_.refs_6_) | copy-start | bytes 2359300
  126.3 1.0 copy-start

commit v2 on v1

v2 whole, which is shorter than its diff:
```python
import jax
import jax.numpy as jnp
from jax import lax
from jax.experimental import pallas as pl
from jax.experimental.pallas import tpu as pltpu
from jax.sharding import Mesh, PartitionSpec as P

HEAD_DIM = 128
LOG2E = 1.4426950408889634
MASKED = -1e30
SCALE = HEAD_DIM ** -0.5 * LOG2E
NX, NZ, NY, NH, NC = 4, 2, 4, 2, 2
XZ, ZY, CTX, MAP = ("x", "zl"), ("zl", "y"), ("x", "zl", "y"), ("x", "zh", "core")
F32, BF16 = jnp.float32, jnp.bfloat16
VMEM_LIMIT = 56 * 1024 * 1024


def nn(a, b):
    return lax.dot_general(a, b, (((1,), (0,)), ((), ())), preferred_element_type=F32)


def nt(a, b):
    return lax.dot_general(a, b, (((1,), (1,)), ((), ())), preferred_element_type=F32)


def pack_kernel(wq_ref, qs_ref, wo_ref, out_ref):
    out_ref[0, 0:256, :] = wq_ref[:, 0:256]
    out_ref[0, 256:512, :] = wq_ref[:, 256:512]
    for block in range(4):
        for part in range(4):
            for half in range(2):
                src = ((block * 4 + part) * 2 + half) * 16
                dst = 512 + ((block * 2 + half) * 4 + part) * 16
                out_ref[0, dst:dst + 16, :] = qs_ref[src:src + 16, :]
    for h in range(4):
        rows = wo_ref[h * 128:(h + 1) * 128, :]
        at = 1024 + (h // 2) * 128
        out_ref[0, at:at + 128, (h % 2) * 128:(h % 2 + 1) * 128] = nt(rows, rows).astype(BF16)


def partial_kernel(got_ref, out_ref):
    for c in range(2):
        acc = jnp.zeros((512, 256), F32)
        for s in range(4):
            acc += nn(got_ref[s, 512:1024, :], got_ref[s, c * 256:(c + 1) * 256, :])
        out_ref[:, :, c * 256:(c + 1) * 256] = acc.reshape(8, 64, 256)
    for pair in range(2):
        gram = jnp.zeros((128, 256), F32)
        for s in range(4):
            gram += got_ref[s, 1024 + pair * 128:1024 + (pair + 1) * 128, :].astype(F32)
        for k in range(2):
            h = 2 * pair + k
            out_ref[2 * h, :, 512:640] = gram[:64, k * 128:(k + 1) * 128]
            out_ref[2 * h + 1, :, 512:640] = gram[64:, k * 128:(k + 1) * 128]


def sum_kernel(got_ref, out_ref):
    total = got_ref[0]
    for k in range(1, 8):
        total += got_ref[k]
    total = total.astype(BF16)
    gram = jnp.concatenate([total[b * 16:(b + 1) * 16, 512:640] for b in range(4)], axis=1)
    for part in range(4):
        for k in range(8):
            out_ref[part, k, 0:16, :] = total[part * 16:(part + 1) * 16, 0:512]
            out_ref[part, k, 16:32, :] = gram


def kv_kernel(k_ref, wk_ref, wv_ref, key_ref, value_ref, acc):
    i = pl.program_id(0)
    k = k_ref[...]
    part = jnp.concatenate([nn(k, wk_ref[...]), nn(k, wv_ref[...])], axis=1)

    @pl.when(i == 0)
    def _():
        acc[...] = part

    @pl.when(i > 0)
    def _():
        acc[...] += part

    @pl.when(i == pl.num_programs(0) - 1)
    def _():
        turned = acc[...].T.astype(BF16)
        key_ref[...] = turned[:256]
        value_ref[...] = turned[256:]


def norm_kernel(value_ref, block_ref, out_ref):
    for h in range(16):
        gram = jnp.concatenate(
            [
                block_ref[2 * (h % 4) + half, h // 4, 16:32, b * 128:(b + 1) * 128]
                for half in range(2)
                for b in range(4)
            ],
            axis=0,
        )
        v = value_ref[(h // 8) * 128:(h // 8 + 1) * 128, :]
        quad = jnp.sum(nn(gram, v) * v.astype(F32), axis=0, keepdims=True)
        out_ref[h // 4, h % 4:h % 4 + 1, :] = jnp.sqrt(jnp.maximum(quad, 0.0) + 1e-6)


def tile_first(info_ref, s):
    return (((info_ref[1] + s) % 4) * 8 + info_ref[2]) * 768


def last_row(info_ref):
    return info_ref[0] + info_ref[1] * 32 + 3 * 128 + 31


def score_tiles(info_ref, q_ref, keys, norms, p_ref, acc, tiles):
    j = pl.program_id(0)
    slab, me = info_ref[0], info_ref[1]
    at = lax.broadcasted_iota(jnp.int32, (128, 128), 1)

    def scored(n, first, masked):
        k = keys[n][...]
        stat = acc[n]
        if masked:
            row = lax.broadcasted_iota(jnp.int32, (128, 1), 0)
            q_pos = slab + (row // 32) * 128 + me * 32 + row % 32
            seen = lax.broadcasted_iota(jnp.int32, (128, 768), 1) <= q_pos - first
        for i in range(4):
            q = q_ref[:, 0, :, i * 128:(i + 1) * 128].reshape(128, 128)
            scores = nn(q, k)
            if masked:
                scores = jnp.where(seen, scores, MASKED)
            peak = jnp.max(scores, axis=1, keepdims=True) * SCALE
            e = jnp.exp2(scores * SCALE - peak)
            p = e * norms[n][0, i:i + 1, :]
            h = 4 * j + i
            stat = jnp.where(at == h, peak, stat)
            stat = jnp.where(at == h + 16, jnp.sum(e, axis=1, keepdims=True), stat)
            stat = jnp.where(at == h + 32, jnp.sum(p, axis=1, keepdims=True), stat)
            p_ref[i, n] = p.astype(BF16)
        acc[n] = stat

    for n, s in enumerate(tiles):
        first = tile_first(info_ref, s)
        full = first + 767 <= slab + me * 32
        none = first > last_row(info_ref)

        @pl.when(full)
        def _():
            scored(n, first, False)

        @pl.when(jnp.logical_not(full) & jnp.logical_not(none))
        def _():
            scored(n, first, True)

        @pl.when(none)
        def _():
            acc[n] = jnp.where(at < 16, MASKED, 0.0)


def own_kernel(info_ref, q_ref, key_ref, norm_ref, p_ref, stat_ref, acc):
    score_tiles(info_ref, q_ref, [key_ref], [norm_ref], p_ref, acc, (0,))

    @pl.when(pl.program_id(0) == 3)
    def _():
        stat_ref[...] = acc[0].T[:48]


def other_kernel(info_ref, q_ref, own_ref, *refs):
    p_ref, stat_ref, peak_ref, acc = refs[6:]
    score_tiles(info_ref, q_ref, refs[0:3], refs[3:6], p_ref, acc, (1, 2, 3))

    @pl.when(pl.program_id(0) == 3)
    def _():
        stats = jnp.stack([own_ref[...]] + [acc[n].T[:48] for n in range(3)])
        peaks = stats[:, 0:16]
        peak = jnp.max(peaks, axis=0)
        factor = jnp.exp2(peaks - peak[None])
        denom = jnp.sum(stats[:, 16:32] * factor, axis=0)
        part = jnp.sum(stats[:, 32:48] * factor, axis=0)
        merged = jnp.concatenate([peak, denom, part], axis=0)
        stat_ref[...] = jnp.broadcast_to(merged[None], (8, 48, 128))
        peak_ref[...] = peaks


def map_kernel(info_ref, own_p_ref, p_ref, peak_ref, all_ref, out_ref, buf, w_scr, sems):
    seen = [tile_first(info_ref, s) <= last_row(info_ref) for s in range(4)]

    def copy(s, part):
        heads = pl.ds(part * 4, 4)
        src = own_p_ref.at[heads, 0] if s == 0 else p_ref.at[heads, s - 1]
        return pltpu.make_async_copy(src, buf.at[s, heads], sems.at[s, part])

    for s in range(4):
        @pl.when(seen[s])
        def _():
            for part in range(4):
                copy(s, part).start()

    peaks = all_ref[:, 0:16, :]
    peak = jnp.max(peaks, axis=0)
    factor = jnp.exp2(peaks - peak[None])
    denom = jnp.sum(all_ref[:, 16:32, :] * factor, axis=0)
    part_sum = jnp.sum(all_ref[:, 32:48, :] * factor, axis=0)
    total = jnp.sum(part_sum / denom, axis=0, keepdims=True)
    for n in range(4):
        weight = jnp.exp2(peak_ref[n] - peak) / denom
        w_scr[n] = jnp.concatenate([weight, total, jnp.zeros((111, 128), F32)], axis=0).T
    total = w_scr[0][:, 16:17]
    high = total.astype(BF16).astype(F32)
    lane = lax.broadcasted_iota(jnp.int32, (128, 128), 1)
    totals = jnp.where(lane == 0, high, jnp.where(lane == 1, total - high, 0.0)).astype(BF16)

    for s in range(4):
        to = (info_ref[1] + s) % 4
        out_ref[pl.ds(to, 1), :, 768:896] = totals[None]

        @pl.when(seen[s])
        def _():
            for part in range(4):
                copy(s, part).wait()
            for r in range(0, 128, 16):
                weights = w_scr[s, r:r + 16, :]
                acc = buf[s, 0, r:r + 16, :].astype(F32) * weights[:, 0:1]
                for h in range(1, 16):
                    acc += buf[s, h, r:r + 16, :].astype(F32) * weights[:, h:h + 1]
                out_ref[pl.ds(to, 1), r:r + 16, 0:768] = acc.astype(BF16)[None]

        @pl.when(jnp.logical_not(seen[s]))
        def _():
            out_ref[pl.ds(to, 1), :, 0:768] = jnp.zeros((1, 128, 768), BF16)


def final_kernel(info_ref, got_ref, out_ref):
    slab, head = info_ref[0], info_ref[3]
    for y in range(4):
        rows = got_ref[4 * y].astype(F32)
        for h in range(1, 4):
            rows += got_ref[4 * y + h].astype(F32)
        total = rows[:, 768:769] + rows[:, 769:770]
        row = lax.broadcasted_iota(jnp.int32, (32, 1), 0)
        pos = (slab + head * 128 + y * 32 + row + 1).astype(F32)
        out_ref[y * 32:(y + 1) * 32, :] = rows[:, :768] * (pos / total)


def from_others(array):
    return [
        lax.ppermute(array, "x", [(i, (i - s) % NX) for i in range(NX)]) for s in (1, 2, 3)
    ]


def local(query_states, key_states, w_query, w_key, w_value, w_out, slab_start):
    x, zl, y = lax.axis_index("x"), lax.axis_index("zl"), lax.axis_index("y")
    head = lax.axis_index("zh") * NC + lax.axis_index("core")
    info = jnp.stack([slab_start[0], x, zl * NY + y, head]).astype(jnp.int32)

    params = pltpu.CompilerParams(vmem_limit_bytes=VMEM_LIMIT)
    vmem = pl.BlockSpec(memory_space=pltpu.VMEM)
    pay = pl.pallas_call(
        pack_kernel,
        out_shape=jax.ShapeDtypeStruct((4, 1280, 256), BF16),
        grid=(4,),
        in_specs=[
            pl.BlockSpec((256, 512), lambda i: (0, i)),
            pl.BlockSpec((512, 256), lambda i: (0, 0)),
            pl.BlockSpec((512, 256), lambda i: (i, 0)),
        ],
        out_specs=pl.BlockSpec((1, 1280, 256), lambda i: (i, 0, 0)),
        compiler_params=params,
        name="pack",
    )(w_query, query_states, w_out)
    got = lax.all_to_all(pay, "y", 0, 0, tiled=True)

    own_keys, own_values = pl.pallas_call(
        kv_kernel,
        out_shape=[jax.ShapeDtypeStruct((256, 768), BF16)] * 2,
        grid=(4,),
        in_specs=[
            pl.BlockSpec((768, 2048), lambda i: (0, i)),
            pl.BlockSpec((2048, 256), lambda i: (i, 0)),
            pl.BlockSpec((2048, 256), lambda i: (i, 0)),
        ],
        out_specs=[pl.BlockSpec((256, 768), lambda i: (0, 0))] * 2,
        scratch_shapes=[pltpu.VMEM((768, 512), F32)],
        compiler_params=params,
        name="project",
    )(key_states, w_key, w_value)
    got, *keys = lax.optimization_barrier((got, *from_others(own_keys)))
    keys = [own_keys] + keys
    parts = pl.pallas_call(
        partial_kernel,
        out_shape=jax.ShapeDtypeStruct((8, 64, 640), F32),
        in_specs=[vmem],
        out_specs=vmem,
        compiler_params=params,
        name="partial",
    )(got)
    parts = lax.all_to_all(parts, XZ, 0, 0, tiled=True)
    block = pl.pallas_call(
        sum_kernel,
        out_shape=jax.ShapeDtypeStruct((4, 8, 32, 512), BF16),
        in_specs=[vmem],
        out_specs=vmem,
        compiler_params=params,
        name="sum",
    )(parts)
    block = lax.all_to_all(block.reshape(32, 32, 512), CTX, 0, 0, tiled=True)
    block = block.reshape(8, 4, 32, 512)

    norms = pl.pallas_call(
        norm_kernel,
        out_shape=jax.ShapeDtypeStruct((4, 4, 768), F32),
        in_specs=[vmem, vmem],
        out_specs=vmem,
        compiler_params=params,
        name="norms",
    )(own_values, block)
    norms = [norms] + from_others(norms)

    q_spec = pl.BlockSpec((8, 1, 16, 512), lambda j, i: (0, j, 0, 0))
    k_spec = pl.BlockSpec((128, 768), lambda j, i: (j // 2, 0))
    n_spec = pl.BlockSpec((1, 4, 768), lambda j, i: (j, 0, 0))
    stat_spec = pl.BlockSpec((48, 128), lambda j, i: (0, 0))
    own_p, own_stats = pl.pallas_call(
        own_kernel,
        out_shape=(
            jax.ShapeDtypeStruct((16, 1, 128, 768), BF16),
            jax.ShapeDtypeStruct((48, 128), F32),
        ),
        grid_spec=pltpu.PrefetchScalarGridSpec(
            num_scalar_prefetch=1,
            grid=(4,),
            in_specs=[q_spec, k_spec, n_spec],
            out_specs=(pl.BlockSpec((4, 1, 128, 768), lambda j, i: (j, 0, 0, 0)), stat_spec),
            scratch_shapes=[pltpu.VMEM((1, 128, 128), F32)],
        ),
        compiler_params=params,
        name="own_scores",
    )(info, block, keys[0], norms[0])
    p, stats, peaks = pl.pallas_call(
        other_kernel,
        out_shape=(
            jax.ShapeDtypeStruct((16, 3, 128, 768), BF16),
            jax.ShapeDtypeStruct((8, 48, 128), F32),
            jax.ShapeDtypeStruct((4, 16, 128), F32),
        ),
        grid_spec=pltpu.PrefetchScalarGridSpec(
            num_scalar_prefetch=1,
            grid=(4,),
            in_specs=[q_spec, stat_spec] + [k_spec] * 3 + [n_spec] * 3,
            out_specs=(
                pl.BlockSpec((4, 3, 128, 768), lambda j, i: (j, 0, 0, 0)),
                pl.BlockSpec((8, 48, 128), lambda j, i: (0, 0, 0)),
                pl.BlockSpec((4, 16, 128), lambda j, i: (0, 0, 0)),
            ),
            scratch_shapes=[pltpu.VMEM((3, 128, 128), F32)],
        ),
        compiler_params=params,
        name="scores",
    )(info, block, own_stats, *keys[1:], *norms[1:])

    all_stats = lax.all_to_all(stats, ZY, 0, 0, tiled=True)

    smem, hbm = pl.BlockSpec(memory_space=pltpu.SMEM), pl.BlockSpec(memory_space=pl.ANY)
    pay = pl.pallas_call(
        map_kernel,
        out_shape=jax.ShapeDtypeStruct((4, 128, 896), BF16),
        in_specs=[smem, hbm, hbm, vmem, vmem],
        out_specs=vmem,
        scratch_shapes=[
            pltpu.VMEM((4, 16, 128, 768), BF16),
            pltpu.VMEM((4, 128, 128), F32),
            pltpu.SemaphoreType.DMA((4, 4)),
        ],
        compiler_params=params,
        name="weigh",
    )(info, own_p, p, peaks, all_stats)
    got = lax.all_to_all(pay.reshape(16, 32, 896), MAP, 0, 0, tiled=True)

    return pl.pallas_call(
        final_kernel,
        out_shape=jax.ShapeDtypeStruct((128, 768), F32),
        in_specs=[
            pl.BlockSpec(memory_space=pltpu.SMEM),
            pl.BlockSpec(memory_space=pltpu.VMEM),
        ],
        out_specs=pl.BlockSpec(memory_space=pltpu.VMEM),
        compiler_params=pltpu.CompilerParams(vmem_limit_bytes=VMEM_LIMIT),
        name="finish",
    )(info, got)


def solution(mesh):
    fine = Mesh(
        mesh.devices.reshape(NX, NZ, NY, NH, NC), ("x", "zl", "y", "zh", "core")
    )
    head = ("zh", "core")
    return jax.shard_map(
        local,
        mesh=fine,
        in_specs=(
            P(None, CTX),
            P(CTX, None),
            P(CTX, head),
            P(None, head),
            P(None, head),
            P(head, CTX),
            P(),
        ),
        out_specs=P(head, CTX),
        check_vma=False,
    )
```

time: 197 us -> 167 us (0.85)
  blocking collectives: 99.1 us -> 60.9 us
  Pallas kernels: 35.8 us -> 54.1 us
  matrix products: 13.8 us -> 0 us
  starting transfers between devices: 8.98 us -> 18.9 us
  local copies, waits for them, and re-layouts: 6.05 us -> 3.18 us
  waiting for transfers between devices: 31.1 us -> 29.1 us
    all_to_all x2 -> x1, blocking collectives: 51.9 us -> 10.9 us  [local(): all_stats = lax.all_to_all(stats, ZY, 0, 0, tiled=True)]
    pallas_call x1 -> x6, Pallas kernels: 21.8 us -> 41 us  [the longest x1 13 us: local(): pl.pallas_call(other_kernel, out_shape=(jax.ShapeDtypeStruct((16, 3, 128,...]
    ppermute x3 -> x6, waiting for transfers between devices: 31.1 us -> 15.7 us  [from_others(): lax.ppermute(array, 'x', [(i, (i - s) % NX) for i in range(NX)])]
    dot_general x1 -> x0, matrix products: 13.8 us -> none  [local(): lax.dot_general(w_kv, key_states, (((0,), (1,)), ((), ())), preferred_ele...]
    all_to_all x1 -> x2, waiting for transfers between devices: 0.01 us -> 13.4 us  [the longest x1 13.4 us: local(): block = lax.all_to_all(block.reshape(32, 32, 512), CTX, 0, 0, tiled=True)]
    all_to_all x1 -> x2, starting transfers between devices: 4.11 us -> 11.2 us  [the longest x1 6.14 us: local(): block = lax.all_to_all(block.reshape(32, 32, 512), CTX, 0, 0, tiled=True)]
    ppermute x3 -> x6, starting transfers between devices: 4.87 us -> 7.77 us  [from_others(): lax.ppermute(array, 'x', [(i, (i - s) % NX) for i in range(NX)])]
    unnamed x11 -> x14, local copies, waits for them, and re-layouts: 1.03 us -> 3.18 us
  transfers between devices with their start and end apart: 4 -> 8, of which waited for: 3 -> 3; matrix products, arithmetic and copies ran while one was open for 7% -> 0% of each run, Pallas kernels for 0% -> 11%
where the time goes in v2:
time: 167 us
  blocking collectives  60.9 us (36%)
  Pallas kernels  54.1 us (32%)
  waiting for transfers between devices  29.1 us (17%)
  starting transfers between devices  18.9 us (11%)
  local copies, waits for them, and re-layouts  3.18 us (2%)
    all_to_all x1, blocking collectives, local(): got = lax.all_to_all(pay.reshape(16, 32, 896), MAP, 0, 0, tiled=True)  27.1 us
    all_to_all x1, blocking collectives, local(): parts = lax.all_to_all(parts, XZ, 0, 0, tiled=True)  22.8 us
    ppermute x6, waiting for transfers between devices, from_others(): lax.ppermute(array, 'x', [(i, (i - s) % NX) for i in range(NX)])  15.7 us
    all_to_all x1, waiting for transfers between devices, local(): block = lax.all_to_all(block.reshape(32, 32, 512), CTX, 0, 0, tiled=True)  13.4 us
    pallas_call x1, Pallas kernels, local(): pl.pallas_call(other_kernel, out_shape=(jax.ShapeDtypeStruct((16, 3, 128,...  13 us
    pallas_call x1, Pallas kernels, local(): pl.pallas_call(kv_kernel, out_shape=[jax.ShapeDtypeStruct((256, 768), BF1...  12 us
    all_to_all x1, blocking collectives, local(): all_stats = lax.all_to_all(stats, ZY, 0, 0, tiled=True)  10.9 us
    ppermute x6, starting transfers between devices, from_others(): lax.ppermute(array, 'x', [(i, (i - s) % NX) for i in range(NX)])  7.77 us
  transfers between devices with their start and end apart: 8, of which 3 were waited for; matrix products, arithmetic and copies ran while one was open for 0% of the time, Pallas kernels for 11%

profile of v2, /device:TPU:1, one launch (start us, length us, event | category | flops | bytes accessed | tf_op | source)
XLA Modules:
  0.0 167.5 jit_solution(402659442399251808)
XLA Ops:
  0.0 4.4 %pack.1 = bf16[4,1280,256]{2,1,0:T(8,128)(2,1)} custom-call(bf16[256,2048]{1,0:T(8,128)(2,1)} %wq_ref.1, bf16[512,256]{1,0:T(8,128)(2,1)} %qs_ref.1, bf16[2048,256]{1,0:T(8,128)(2,1)} %wo_ref.1), custom_call_target="tpu_custom_call" | custom-call | tf_op jit(solution)/shard_map/pack/pallas_call | solution.py:255
  4.4 5.0 %all-to-all-start = ((bf16[4,1280,256]{2,1,0:T(8,128)(2,1)}), bf16[4,1280,256]{2,1,0:T(8,128)(2,1)S(1)}, u32[]{:S(2)}, u32[]{:S(2)}) async-start(bf16[4,1280,256]{2,1,0:T(8,128)(2,1)} %pack.1), calls=%async_computation | async-start | bytes 5242880 | tf_op jit(solution)/shard_map/all_to_all | solution.py:268
  9.4 12.0 %project.1 = (bf16[256,768]{1,0:T(8,128)(2,1)}, bf16[256,768]{1,0:T(8,128)(2,1)}) custom-call(bf16[768,8192]{1,0:T(8,128)(2,1)} %k_ref.1, bf16[8192,256]{1,0:T(8,128)(2,1)} %wk_ref.1, bf16[8192,256]{1,0:T(8,128)(2,1)} %wv_ref.1), custom_call_target="tpu_custom_call" | custom-call | tf_op jit(solution)/shard_map/project/pallas_call | solution.py:270
  21.4 1.2 collective-permute-start.2
  22.6 2.5 %collective-permute-start.1 = (bf16[256,768]{1,0:T(8,128)(2,1)}, bf16[256,768]{1,0:T(8,128)(2,1)S(1)}, u32[]{:S(2)}, u32[]{:S(2)}) collective-permute-start(bf16[256,768]{1,0:T(8,128)(2,1)} %get-tuple-element.16.key_ref), channel_id=1, source_target_pairs={{0,64},{32,96},{64,0},{96,32},{1,65},{33,97},{65,1},{97,33},{2,66}... | collective-permute-start | bytes 1179656 | tf_op jit(solution)/shard_map/ppermute | solution.py:244
  25.0 1.1 collective-permute-start
  26.2 6.3 %collective-permute-done.2.refs_2_ = bf16[256,768]{1,0:T(8,128)(2,1)S(1)} collective-permute-done((bf16[256,768]{1,0:T(8,128)(2,1)}, bf16[256,768]{1,0:T(8,128)(2,1)S(1)}, u32[]{:S(2)}, u32[]{:S(2)}) %collective-permute-start.2) | collective-permute-done | bytes 393248 | tf_op jit(solution)/shard_map/ppermute | solution.py:244
  32.4 9.4 %collective-permute-done.1.refs_1_ = bf16[256,768]{1,0:T(8,128)(2,1)S(1)} collective-permute-done((bf16[256,768]{1,0:T(8,128)(2,1)}, bf16[256,768]{1,0:T(8,128)(2,1)S(1)}, u32[]{:S(2)}, u32[]{:S(2)}) %collective-permute-start.1) | collective-permute-done | bytes 393248 | tf_op jit(solution)/shard_map/ppermute | solution.py:244
  41.9 0.0 collective-permute-done.refs_0_
  41.9 0.0 all-to-all-done.got_ref
  41.9 1.5 copy-done.1
  43.5 3.5 %partial.1 = f32[8,64,640]{2,1,0:T(8,128)} custom-call(bf16[4,1280,256]{2,1,0:T(8,128)(2,1)} %copy-done.1), custom_call_target="tpu_custom_call" | custom-call | tf_op jit(solution)/shard_map/partial/pallas_call | solution.py:286
  47.0 22.8 %all_to_all.25.got_ref = f32[8,64,640]{2,1,0:T(8,128)} all-to-all(f32[8,64,640]{2,1,0:T(8,128)} %partial.1), channel_id=1, replica_groups=mesh['x'=4,'zl'=2,'y'=4,'zh'=2,'core'=2] {'x','zl'}, dimensions={0} | all-to-all | bytes 2621440 | tf_op jit(solution)/shard_map/all_to_all | solution.py:294
  69.8 2.4 %sum.1 = bf16[4,8,32,512]{3,2,1,0:T(8,128)(2,1)} custom-call(f32[8,64,640]{2,1,0:T(8,128)} %all_to_all.25.got_ref), custom_call_target="tpu_custom_call" | custom-call | tf_op jit(solution)/shard_map/sum/pallas_call | solution.py:295
  72.2 6.1 %all-to-all-start.2 = ((bf16[32,32,512]{2,1,0:T(8,128)(2,1)}), bf16[32,32,512]{2,1,0:T(8,128)(2,1)S(1)}, u32[]{:S(2)}, u32[]{:S(2)}) async-start(bf16[32,32,512]{2,1,0:T(8,128)(2,1)} %bitcast.9), calls=%async_computation.2 | async-start | bytes 2097152 | tf_op jit(solution)/shard_map/all_to_all | solution.py:303
  79.0 13.4 %all-to-all-done.2 = bf16[32,32,512]{2,1,0:T(8,128)(2,1)S(1)} async-done(((bf16[32,32,512]{2,1,0:T(8,128)(2,1)}), bf16[32,32,512]{2,1,0:T(8,128)(2,1)S(1)}, u32[]{:S(2)}, u32[]{:S(2)}) %all-to-all-start.2) | async-done | bytes 1048608 | tf_op jit(solution)/shard_map/all_to_all | solution.py:303
  92.4 1.0 copy-done
  93.4 3.0 %norms.1.norm_ref = f32[4,4,768]{2,1,0:T(4,128)} custom-call(bf16[256,768]{1,0:T(8,128)(2,1)} %get-tuple-element.18.value_ref, bf16[8,4,32,512]{3,2,1,0:T(8,128)(2,1)} %bitcast.6), custom_call_target="tpu_custom_call" | custom-call | tf_op jit(solution)/shard_map/norms/pallas_call | solution.py:306
  96.4 0.0 collective-permute-start.5
  96.4 2.6 %collective-permute-start.4 = (f32[4,4,768]{2,1,0:T(4,128)}, f32[4,4,768]{2,1,0:T(4,128)S(1)}, u32[]{:S(2)}, u32[]{:S(2)}) collective-permute-start(f32[4,4,768]{2,1,0:T(4,128)} %norms.1.norm_ref), channel_id=1, source_target_pairs={{0,64},{32,96},{64,0},{96,32},{1,65},{33,97},{65,1},{97,33},{2,66}... | collective-permute-start | bytes 147464 | tf_op jit(solution)/shard_map/ppermute | solution.py:244
  99.0 0.4 collective-permute-start.3
  99.4 0.6 pad_add_fusion.info_ref
  100.0 6.3 %own_scores.1 = (bf16[16,1,128,768]{3,2,1,0:T(8,128)(2,1)}, f32[48,128]{1,0:T(8,128)}) custom-call(s32[4]{0:T(128)} %pad_add_fusion.info_ref, bf16[8,4,32,512]{3,2,1,0:T(8,128)(2,1)} %bitcast.7, bf16[256,768]{1,0:T(8,128)(2,1)} %get-tuple-element.16.key_ref, f32[4,4,768]{2,1,0:T(4,128)} %norms.1.norm_ref), custom_call_target="tpu_custom_call" | custom-call | tf_op jit(solution)/shard_map/own_scores/pallas_call | solution.py:320
  106.3 0.0 collective-permute-done.5.refs_5_
  106.4 0.6 copy-done.4
  106.9 0.0 copy-done.5
  106.9 0.0 copy-done.6
  107.0 13.0 %scores.1 = (bf16[16,3,128,768]{3,2,1,0:T(8,128)(2,1)}, f32[8,48,128]{2,1,0:T(8,128)}, f32[4,16,128]{2,1,0:T(8,128)}) custom-call(s32[4]{0:T(128)} %pad_add_fusion.info_ref, bf16[8,4,32,512]{3,2,1,0:T(8,128)(2,1)} %bitcast.8, f32[48,128]{1,0:T(8,128)} %get-tuple-element.20.own_ref, bf16[256,768]{1,0:T(8,128)(2,1)} %collective-permute-done.refs_0_, ...), custom_call_target="tpu_custom_call" | custom-call | tf_op jit(solution)/shard_map/scores/pallas_call | solution.py:336
  119.9 10.9 %all_to_all.26.all_ref = f32[8,48,128]{2,1,0:T(8,128)} all-to-all(f32[8,48,128]{2,1,0:T(8,128)} %get-tuple-element.26), channel_id=1, replica_groups=mesh['x'=4,'zl'=2,'y'=4,'zh'=2,'core'=2] {'zl','y'}, dimensions={0} | all-to-all | bytes 393216 | tf_op jit(solution)/shard_map/all_to_all | solution.py:358
  130.9 7.4 %weigh.1 = bf16[4,128,896]{2,1,0:T(8,128)(2,1)} custom-call(s32[4]{0:T(128)} %pad_add_fusion.info_ref, bf16[16,1,128,768]{3,2,1,0:T(8,128)(2,1)} %get-tuple-element.19.own_p_ref, bf16[16,3,128,768]{3,2,1,0:T(8,128)(2,1)} %get-tuple-element.24.p_ref, f32[4,16,128]{2,1,0:T(8,128)} %get-tuple-element.25.peak_ref, f32[8,48,128]{2,1,0:T(8,128)} %all_to_all.26.all_ref), custom_call_target="tpu_custom_call" | custom-call | tf_op jit(solution)/shard_map/weigh/pallas_call | solution.py:361
  138.3 27.1 %all_to_all.27.got_ref = bf16[16,32,896]{2,1,0:T(8,128)(2,1)} all-to-all(bf16[16,32,896]{2,1,0:T(8,128)(2,1)} %bitcast.10), channel_id=1, replica_groups=mesh['x'=4,'zl'=2,'y'=4,'zh'=2,'core'=2] {'x','zh','core'}, dimensions={0} | all-to-all | bytes 1835008 | tf_op jit(solution)/shard_map/all_to_all | solution.py:374
  165.4 2.1 %finish.1 = f32[128,768]{1,0:T(8,128)} custom-call(s32[4]{0:T(128)} %pad_add_fusion.info_ref, bf16[16,32,896]{2,1,0:T(8,128)(2,1)} %all_to_all.27.got_ref), custom_call_target="tpu_custom_call" | custom-call | tf_op jit(solution)/shard_map/finish/pallas_call | solution.py:376
  (11 shorter events, 0.0 us)
Async XLA Ops:
  4.4 37.6 %all-to-all-start = ((bf16[4,1280,256]{2,1,0:T(8,128)(2,1)}), bf16[4,1280,256]{2,1,0:T(8,128)(2,1)S(1)}, u32[]{:S(2)}, u32[]{:S(2)}) async-start(bf16[4,1280,256]{2,1,0:T(8,128)(2,1)} %pack.1), calls=%async_computation | async-start | bytes 5242880 | tf_op jit(solution)/shard_map/all_to_all | solution.py:268
  21.4 11.1 %collective-permute-start.2 = (bf16[256,768]{1,0:T(8,128)(2,1)}, bf16[256,768]{1,0:T(8,128)(2,1)S(1)}, u32[]{:S(2)}, u32[]{:S(2)}) collective-permute-start(bf16[256,768]{1,0:T(8,128)(2,1)} %get-tuple-element.16.key_ref), channel_id=1, source_target_pairs={{0,32},{32,64},{64,96},{96,0},{1,33},{33,65},{65,97},{97,1},{2,34}... | collective-permute-start | bytes 1179656 | tf_op jit(solution)/shard_map/ppermute | solution.py:244
  22.6 19.3 %collective-permute-start.1 = (bf16[256,768]{1,0:T(8,128)(2,1)}, bf16[256,768]{1,0:T(8,128)(2,1)S(1)}, u32[]{:S(2)}, u32[]{:S(2)}) collective-permute-start(bf16[256,768]{1,0:T(8,128)(2,1)} %get-tuple-element.16.key_ref), channel_id=1, source_target_pairs={{0,64},{32,96},{64,0},{96,32},{1,65},{33,97},{65,1},{97,33},{2,66}... | collective-permute-start | bytes 1179656 | tf_op jit(solution)/shard_map/ppermute | solution.py:244
  25.0 16.9 %collective-permute-start = (bf16[256,768]{1,0:T(8,128)(2,1)}, bf16[256,768]{1,0:T(8,128)(2,1)}, u32[]{:S(2)}, u32[]{:S(2)}) collective-permute-start(bf16[256,768]{1,0:T(8,128)(2,1)} %get-tuple-element.16.key_ref), channel_id=1, source_target_pairs={{0,96},{32,0},{64,32},{96,64},{1,97},{33,1},{65,33},{97,65},{2,98}... | collective-permute-start | bytes 1179656 | tf_op jit(solution)/shard_map/ppermute | solution.py:244
  32.4 73.9 %copy-start.2 = (bf16[256,768]{1,0:T(8,128)(2,1)}, bf16[256,768]{1,0:T(8,128)(2,1)S(1)}, u32[]{:S(2)}) copy-start(bf16[256,768]{1,0:T(8,128)(2,1)S(1)} %collective-permute-done.2.refs_2_) | copy-start | bytes 1179652
  41.9 64.5 %copy-start.3 = (bf16[256,768]{1,0:T(8,128)(2,1)}, bf16[256,768]{1,0:T(8,128)(2,1)S(1)}, u32[]{:S(2)}) copy-start(bf16[256,768]{1,0:T(8,128)(2,1)S(1)} %collective-permute-done.1.refs_1_) | copy-start | bytes 1179652
  41.9 1.5 copy-start.1
  72.2 20.2 %all-to-all-start.2 = ((bf16[32,32,512]{2,1,0:T(8,128)(2,1)}), bf16[32,32,512]{2,1,0:T(8,128)(2,1)S(1)}, u32[]{:S(2)}, u32[]{:S(2)}) async-start(bf16[32,32,512]{2,1,0:T(8,128)(2,1)} %bitcast.9), calls=%async_computation.2 | async-start | bytes 2097152 | tf_op jit(solution)/shard_map/all_to_all | solution.py:303
  92.4 1.0 copy-start
  96.4 9.9 %collective-permute-start.5 = (f32[4,4,768]{2,1,0:T(4,128)}, f32[4,4,768]{2,1,0:T(4,128)S(1)}, u32[]{:S(2)}, u32[]{:S(2)}) collective-permute-start(f32[4,4,768]{2,1,0:T(4,128)} %norms.1.norm_ref), channel_id=1, source_target_pairs={{0,32},{32,64},{64,96},{96,0},{1,33},{33,65},{65,97},{97,1},{2,34}... | collective-permute-start | bytes 147464 | tf_op jit(solution)/shard_map/ppermute | solution.py:244
  96.4 9.9 %collective-permute-start.4 = (f32[4,4,768]{2,1,0:T(4,128)}, f32[4,4,768]{2,1,0:T(4,128)S(1)}, u32[]{:S(2)}, u32[]{:S(2)}) collective-permute-start(f32[4,4,768]{2,1,0:T(4,128)} %norms.1.norm_ref), channel_id=1, source_target_pairs={{0,64},{32,96},{64,0},{96,32},{1,65},{33,97},{65,1},{97,33},{2,66}... | collective-permute-start | bytes 147464 | tf_op jit(solution)/shard_map/ppermute | solution.py:244
  99.0 7.3 %collective-permute-start.3 = (f32[4,4,768]{2,1,0:T(4,128)}, f32[4,4,768]{2,1,0:T(4,128)S(1)}, u32[]{:S(2)}, u32[]{:S(2)}) collective-permute-start(f32[4,4,768]{2,1,0:T(4,128)} %norms.1.norm_ref), channel_id=1, source_target_pairs={{0,96},{32,0},{64,32},{96,64},{1,97},{33,1},{65,33},{97,65},{2,98}... | collective-permute-start | bytes 147464 | tf_op jit(solution)/shard_map/ppermute | solution.py:244
  106.3 0.6 copy-start.4
  106.3 0.6 copy-start.5
  106.3 0.6 copy-start.6

commit v3 on v2

--- a/solution.py
+++ b/solution.py
@@ -66,10 +66,9 @@
             out_ref[part, k, 16:32, :] = gram
 
 
-def kv_kernel(k_ref, wk_ref, wv_ref, key_ref, value_ref, acc):
+def project_kernel(state_ref, w_ref, out_ref, acc):
     i = pl.program_id(0)
-    k = k_ref[...]
-    part = jnp.concatenate([nn(k, wk_ref[...]), nn(k, wv_ref[...])], axis=1)
+    part = nn(state_ref[...], w_ref[...])
 
     @pl.when(i == 0)
     def _():
@@ -81,9 +80,23 @@
 
     @pl.when(i == pl.num_programs(0) - 1)
     def _():
-        turned = acc[...].T.astype(BF16)
-        key_ref[...] = turned[:256]
-        value_ref[...] = turned[256:]
+        out_ref[...] = acc[...].T.astype(BF16)
+
+
+def project(states, weights, name):
+    return pl.pallas_call(
+        project_kernel,
+        out_shape=jax.ShapeDtypeStruct((256, 768), BF16),
+        grid=(4,),
+        in_specs=[
+            pl.BlockSpec((768, 2048), lambda i: (0, i)),
+            pl.BlockSpec((2048, 256), lambda i: (i, 0)),
+        ],
+        out_specs=pl.BlockSpec((256, 768), lambda i: (0, 0)),
+        scratch_shapes=[pltpu.VMEM((768, 256), F32)],
+        compiler_params=pltpu.CompilerParams(vmem_limit_bytes=VMEM_LIMIT),
+        name=name,
+    )(states, weights)
 
 
 def norm_kernel(value_ref, block_ref, out_ref):
@@ -267,21 +280,11 @@
     )(w_query, query_states, w_out)
     got = lax.all_to_all(pay, "y", 0, 0, tiled=True)
 
-    own_keys, own_values = pl.pallas_call(
-        kv_kernel,
-        out_shape=[jax.ShapeDtypeStruct((256, 768), BF16)] * 2,
-        grid=(4,),
-        in_specs=[
-            pl.BlockSpec((768, 2048), lambda i: (0, i)),
-            pl.BlockSpec((2048, 256), lambda i: (i, 0)),
-            pl.BlockSpec((2048, 256), lambda i: (i, 0)),
-        ],
-        out_specs=[pl.BlockSpec((256, 768), lambda i: (0, 0))] * 2,
-        scratch_shapes=[pltpu.VMEM((768, 512), F32)],
-        compiler_params=params,
-        name="project",
-    )(key_states, w_key, w_value)
-    got, *keys = lax.optimization_barrier((got, *from_others(own_keys)))
+    own_keys = project(key_states, w_key, "project_keys")
+    own_values = project(key_states, w_value, "project_values")
+    got, info, own_values, *keys = lax.optimization_barrier(
+        (got, info, own_values, *from_others(own_keys))
+    )
     keys = [own_keys] + keys
     parts = pl.pallas_call(
         partial_kernel,

time: 167 us -> 162 us (0.970)
  waiting for transfers between devices: 29.1 us -> 7.31 us
  blocking collectives: 60.9 us -> 79.5 us
  starting transfers between devices: 18.9 us -> 12.8 us
  Pallas kernels: 54.1 us -> 59.6 us
    all_to_all x0 -> x1, blocking collectives: none -> 20.4 us  [local(): block = lax.all_to_all(block.reshape(32, 32, 512), CTX, 0, 0, tiled=True)]
    all_to_all x1 -> x0, waiting for transfers between devices: 13.4 us -> none  [local(): block = lax.all_to_all(block.reshape(32, 32, 512), CTX, 0, 0, tiled=True)]
    ppermute x6, waiting for transfers between devices: 15.7 us -> 5.62 us  [from_others(): lax.ppermute(array, 'x', [(i, (i - s) % NX) for i in range(NX)])]
    all_to_all x1 -> x0, starting transfers between devices: 6.14 us -> none  [local(): block = lax.all_to_all(block.reshape(32, 32, 512), CTX, 0, 0, tiled=True)]
    pallas_call x1 -> x2, Pallas kernels: 12 us -> 17.6 us  [project(): pl.pallas_call(project_kernel, out_shape=jax.ShapeDtypeStruct((256, 768),...]
    all_to_all x1, blocking collectives: 22.8 us -> 21.1 us  [local(): parts = lax.all_to_all(parts, XZ, 0, 0, tiled=True)]
    all_to_all x1, waiting for transfers between devices: 0.01 us -> 1.69 us  [local(): got = lax.all_to_all(pay, 'y', 0, 0, tiled=True)]
  transfers between devices with their start and end apart: 8 -> 7, of which waited for: 3 -> 3; matrix products, arithmetic and copies ran while one was open for 0% -> 0% of each run, Pallas kernels for 11% -> 15%
where the time goes in v3:
time: 162 us; the launch traced here: 163 us
  blocking collectives  79.5 us (49%)
  Pallas kernels  59.6 us (37%)
  starting transfers between devices  12.8 us (8%)
  waiting for transfers between devices  7.31 us (5%)
  local copies, waits for them, and re-layouts  2.1 us (1%)
    all_to_all x1, blocking collectives, local(): got = lax.all_to_all(pay.reshape(16, 32, 896), MAP, 0, 0, tiled=True)  27.6 us
    all_to_all x1, blocking collectives, local(): parts = lax.all_to_all(parts, XZ, 0, 0, tiled=True)  21.1 us
    all_to_all x1, blocking collectives, local(): block = lax.all_to_all(block.reshape(32, 32, 512), CTX, 0, 0, tiled=True)  20.4 us
    pallas_call x2, Pallas kernels, project(): pl.pallas_call(project_kernel, out_shape=jax.ShapeDtypeStruct((256, 768),...  17.6 us
    pallas_call x1, Pallas kernels, local(): pl.pallas_call(other_kernel, out_shape=(jax.ShapeDtypeStruct((16, 3, 128,...  13 us
    all_to_all x1, blocking collectives, local(): all_stats = lax.all_to_all(stats, ZY, 0, 0, tiled=True)  10.5 us
    ppermute x6, starting transfers between devices, from_others(): lax.ppermute(array, 'x', [(i, (i - s) % NX) for i in range(NX)])  7.76 us
    pallas_call x1, Pallas kernels, local(): pl.pallas_call(map_kernel, out_shape=jax.ShapeDtypeStruct((4, 128, 896),...  7.39 us
  transfers between devices with their start and end apart: 7, of which 3 were waited for; matrix products, arithmetic and copies ran while one was open for 0% of the time, Pallas kernels for 15%

profile of v3, /device:TPU:1, one launch (start us, length us, event | category | flops | bytes accessed | tf_op | source)
XLA Modules:
  0.0 162.7 jit_solution(13008794239281333678)
XLA Ops:
  0.0 4.3 %pack.1 = bf16[4,1280,256]{2,1,0:T(8,128)(2,1)} custom-call(bf16[256,2048]{1,0:T(8,128)(2,1)} %wq_ref.1, bf16[512,256]{1,0:T(8,128)(2,1)} %qs_ref.1, bf16[2048,256]{1,0:T(8,128)(2,1)} %wo_ref.1), custom_call_target="tpu_custom_call" | custom-call | tf_op jit(solution)/shard_map/pack/pallas_call | solution.py:268
  4.3 5.0 %all-to-all-start = ((bf16[4,1280,256]{2,1,0:T(8,128)(2,1)}), bf16[4,1280,256]{2,1,0:T(8,128)(2,1)S(1)}, u32[]{:S(2)}, u32[]{:S(2)}) async-start(bf16[4,1280,256]{2,1,0:T(8,128)(2,1)} %pack.1), calls=%async_computation | async-start | bytes 5242880 | tf_op jit(solution)/shard_map/all_to_all | solution.py:281
  9.4 8.8 %project_keys.1.key_ref = bf16[256,768]{1,0:T(8,128)(2,1)} custom-call(bf16[768,8192]{1,0:T(8,128)(2,1)} %state_ref.3, bf16[8192,256]{1,0:T(8,128)(2,1)} %w_ref.3), custom_call_target="tpu_custom_call" | custom-call | tf_op jit(solution)/shard_map/project_keys/pallas_call | solution.py:87
  18.2 1.2 collective-permute-start.2
  19.4 2.5 %collective-permute-start.1 = (bf16[256,768]{1,0:T(8,128)(2,1)}, bf16[256,768]{1,0:T(8,128)(2,1)S(1)}, u32[]{:S(2)}, u32[]{:S(2)}) collective-permute-start(bf16[256,768]{1,0:T(8,128)(2,1)} %project_keys.1.key_ref), channel_id=1, source_target_pairs={{0,64},{32,96},{64,0},{96,32},{1,65},{33,97},{65,1},{97,33},{2,66}... | collective-permute-start | bytes 1179656 | tf_op jit(solution)/shard_map/ppermute | solution.py:257
  21.8 1.2 collective-permute-start
  23.6 8.8 %project_values.1.value_ref = bf16[256,768]{1,0:T(8,128)(2,1)} custom-call(bf16[768,8192]{1,0:T(8,128)(2,1)} %state_ref.3, bf16[8192,256]{1,0:T(8,128)(2,1)} %w_ref.2), custom_call_target="tpu_custom_call" | custom-call | tf_op jit(solution)/shard_map/project_values/pallas_call | solution.py:87
  32.5 0.6 pad_add_fusion.info_ref
  33.1 0.0 collective-permute-done.2.refs_2_
  33.1 5.6 %collective-permute-done.1.refs_1_ = bf16[256,768]{1,0:T(8,128)(2,1)S(1)} collective-permute-done((bf16[256,768]{1,0:T(8,128)(2,1)}, bf16[256,768]{1,0:T(8,128)(2,1)S(1)}, u32[]{:S(2)}, u32[]{:S(2)}) %collective-permute-start.1) | collective-permute-done | bytes 393248 | tf_op jit(solution)/shard_map/ppermute | solution.py:257
  38.7 0.1 collective-permute-done.refs_0_
  38.7 1.7 %all-to-all-done.got_ref = bf16[4,1280,256]{2,1,0:T(8,128)(2,1)S(1)} async-done(((bf16[4,1280,256]{2,1,0:T(8,128)(2,1)}), bf16[4,1280,256]{2,1,0:T(8,128)(2,1)S(1)}, u32[]{:S(2)}, u32[]{:S(2)}) %all-to-all-start) | async-done | bytes 2621472 | tf_op jit(solution)/shard_map/all_to_all | solution.py:281
  40.4 1.5 copy-done
  41.9 3.5 %partial.1 = f32[8,64,640]{2,1,0:T(8,128)} custom-call(bf16[4,1280,256]{2,1,0:T(8,128)(2,1)} %copy-done), custom_call_target="tpu_custom_call" | custom-call | tf_op jit(solution)/shard_map/partial/pallas_call | solution.py:289
  45.4 21.1 %all_to_all.25.got_ref = f32[8,64,640]{2,1,0:T(8,128)} all-to-all(f32[8,64,640]{2,1,0:T(8,128)} %partial.1), channel_id=1, replica_groups=mesh['x'=4,'zl'=2,'y'=4,'zh'=2,'core'=2] {'x','zl'}, dimensions={0} | all-to-all | bytes 2621440 | tf_op jit(solution)/shard_map/all_to_all | solution.py:297
  66.5 2.4 %sum.1 = bf16[4,8,32,512]{3,2,1,0:T(8,128)(2,1)} custom-call(f32[8,64,640]{2,1,0:T(8,128)} %all_to_all.25.got_ref), custom_call_target="tpu_custom_call" | custom-call | tf_op jit(solution)/shard_map/sum/pallas_call | solution.py:298
  68.9 20.4 %all_to_all.26 = bf16[32,32,512]{2,1,0:T(8,128)(2,1)} all-to-all(bf16[32,32,512]{2,1,0:T(8,128)(2,1)} %bitcast.9), channel_id=1, replica_groups=mesh['x'=4,'zl'=2,'y'=4,'zh'=2,'core'=2] {'x','zl','y'}, dimensions={0} | all-to-all | bytes 2097152 | tf_op jit(solution)/shard_map/all_to_all | solution.py:306
  89.3 3.0 %norms.1.norm_ref = f32[4,4,768]{2,1,0:T(4,128)} custom-call(bf16[256,768]{1,0:T(8,128)(2,1)} %project_values.1.value_ref, bf16[8,4,32,512]{3,2,1,0:T(8,128)(2,1)} %bitcast.6), custom_call_target="tpu_custom_call" | custom-call | tf_op jit(solution)/shard_map/norms/pallas_call | solution.py:309
  92.3 0.0 collective-permute-start.5
  92.3 2.5 %collective-permute-start.4 = (f32[4,4,768]{2,1,0:T(4,128)}, f32[4,4,768]{2,1,0:T(4,128)S(1)}, u32[]{:S(2)}, u32[]{:S(2)}) collective-permute-start(f32[4,4,768]{2,1,0:T(4,128)} %norms.1.norm_ref), channel_id=1, source_target_pairs={{0,64},{32,96},{64,0},{96,32},{1,65},{33,97},{65,1},{97,33},{2,66}... | collective-permute-start | bytes 147464 | tf_op jit(solution)/shard_map/ppermute | solution.py:257
  94.8 0.4 collective-permute-start.3
  95.3 6.3 %own_scores.1 = (bf16[16,1,128,768]{3,2,1,0:T(8,128)(2,1)}, f32[48,128]{1,0:T(8,128)}) custom-call(s32[4]{0:T(128)} %pad_add_fusion.info_ref, bf16[8,4,32,512]{3,2,1,0:T(8,128)(2,1)} %bitcast.7, bf16[256,768]{1,0:T(8,128)(2,1)} %project_keys.1.key_ref, f32[4,4,768]{2,1,0:T(4,128)} %norms.1.norm_ref), custom_call_target="tpu_custom_call" | custom-call | tf_op jit(solution)/shard_map/own_scores/pallas_call | solution.py:323
  101.5 0.0 collective-permute-done.5.refs_5_
  101.6 0.0 collective-permute-done.3.refs_3_
  101.6 0.6 copy-done.3
  102.2 0.0 copy-done.4
  102.2 0.0 copy-done.5
  102.2 13.0 %scores.1 = (bf16[16,3,128,768]{3,2,1,0:T(8,128)(2,1)}, f32[8,48,128]{2,1,0:T(8,128)}, f32[4,16,128]{2,1,0:T(8,128)}) custom-call(s32[4]{0:T(128)} %pad_add_fusion.info_ref, bf16[8,4,32,512]{3,2,1,0:T(8,128)(2,1)} %bitcast.8, f32[48,128]{1,0:T(8,128)} %get-tuple-element.20.own_ref, bf16[256,768]{1,0:T(8,128)(2,1)} %collective-permute-done.refs_0_, ...), custom_call_target="tpu_custom_call" | custom-call | tf_op jit(solution)/shard_map/scores/pallas_call | solution.py:339
  115.2 10.5 %all_to_all.27.all_ref = f32[8,48,128]{2,1,0:T(8,128)} all-to-all(f32[8,48,128]{2,1,0:T(8,128)} %get-tuple-element.26), channel_id=1, replica_groups=mesh['x'=4,'zl'=2,'y'=4,'zh'=2,'core'=2] {'zl','y'}, dimensions={0} | all-to-all | bytes 393216 | tf_op jit(solution)/shard_map/all_to_all | solution.py:361
  125.6 7.4 %weigh.1 = bf16[4,128,896]{2,1,0:T(8,128)(2,1)} custom-call(s32[4]{0:T(128)} %pad_add_fusion.info_ref, bf16[16,1,128,768]{3,2,1,0:T(8,128)(2,1)} %get-tuple-element.19.own_p_ref, bf16[16,3,128,768]{3,2,1,0:T(8,128)(2,1)} %get-tuple-element.24.p_ref, f32[4,16,128]{2,1,0:T(8,128)} %get-tuple-element.25.peak_ref, f32[8,48,128]{2,1,0:T(8,128)} %all_to_all.27.all_ref), custom_call_target="tpu_custom_call" | custom-call | tf_op jit(solution)/shard_map/weigh/pallas_call | solution.py:364
  133.0 27.6 %all_to_all.28.got_ref = bf16[16,32,896]{2,1,0:T(8,128)(2,1)} all-to-all(bf16[16,32,896]{2,1,0:T(8,128)(2,1)} %bitcast.10), channel_id=1, replica_groups=mesh['x'=4,'zl'=2,'y'=4,'zh'=2,'core'=2] {'x','zh','core'}, dimensions={0} | all-to-all | bytes 1835008 | tf_op jit(solution)/shard_map/all_to_all | solution.py:377
  160.6 2.1 %finish.1 = f32[128,768]{1,0:T(8,128)} custom-call(s32[4]{0:T(128)} %pad_add_fusion.info_ref, bf16[16,32,896]{2,1,0:T(8,128)(2,1)} %all_to_all.28.got_ref), custom_call_target="tpu_custom_call" | custom-call | tf_op jit(solution)/shard_map/finish/pallas_call | solution.py:379
  (9 shorter events, 0.0 us)
Async XLA Ops:
  4.3 36.1 %all-to-all-start = ((bf16[4,1280,256]{2,1,0:T(8,128)(2,1)}), bf16[4,1280,256]{2,1,0:T(8,128)(2,1)S(1)}, u32[]{:S(2)}, u32[]{:S(2)}) async-start(bf16[4,1280,256]{2,1,0:T(8,128)(2,1)} %pack.1), calls=%async_computation | async-start | bytes 5242880 | tf_op jit(solution)/shard_map/all_to_all | solution.py:281
  18.2 14.9 %collective-permute-start.2 = (bf16[256,768]{1,0:T(8,128)(2,1)}, bf16[256,768]{1,0:T(8,128)(2,1)S(1)}, u32[]{:S(2)}, u32[]{:S(2)}) collective-permute-start(bf16[256,768]{1,0:T(8,128)(2,1)} %project_keys.1.key_ref), channel_id=1, source_target_pairs={{0,32},{32,64},{64,96},{96,0},{1,33},{33,65},{65,97},{97,1},{2,34}... | collective-permute-start | bytes 1179656 | tf_op jit(solution)/shard_map/ppermute | solution.py:257
  19.4 19.3 %collective-permute-start.1 = (bf16[256,768]{1,0:T(8,128)(2,1)}, bf16[256,768]{1,0:T(8,128)(2,1)S(1)}, u32[]{:S(2)}, u32[]{:S(2)}) collective-permute-start(bf16[256,768]{1,0:T(8,128)(2,1)} %project_keys.1.key_ref), channel_id=1, source_target_pairs={{0,64},{32,96},{64,0},{96,32},{1,65},{33,97},{65,1},{97,33},{2,66}... | collective-permute-start | bytes 1179656 | tf_op jit(solution)/shard_map/ppermute | solution.py:257
  21.8 16.9 %collective-permute-start = (bf16[256,768]{1,0:T(8,128)(2,1)}, bf16[256,768]{1,0:T(8,128)(2,1)}, u32[]{:S(2)}, u32[]{:S(2)}) collective-permute-start(bf16[256,768]{1,0:T(8,128)(2,1)} %project_keys.1.key_ref), channel_id=1, source_target_pairs={{0,96},{32,0},{64,32},{96,64},{1,97},{33,1},{65,33},{97,65},{2,98}... | collective-permute-start | bytes 1179656 | tf_op jit(solution)/shard_map/ppermute | solution.py:257
  33.1 68.5 %copy-start.1 = (bf16[256,768]{1,0:T(8,128)(2,1)}, bf16[256,768]{1,0:T(8,128)(2,1)S(1)}, u32[]{:S(2)}) copy-start(bf16[256,768]{1,0:T(8,128)(2,1)S(1)} %collective-permute-done.2.refs_2_) | copy-start | bytes 1179652
  38.7 63.0 %copy-start.2 = (bf16[256,768]{1,0:T(8,128)(2,1)}, bf16[256,768]{1,0:T(8,128)(2,1)S(1)}, u32[]{:S(2)}) copy-start(bf16[256,768]{1,0:T(8,128)(2,1)S(1)} %collective-permute-done.1.refs_1_) | copy-start | bytes 1179652
  40.4 1.5 copy-start
  92.3 9.2 %collective-permute-start.5 = (f32[4,4,768]{2,1,0:T(4,128)}, f32[4,4,768]{2,1,0:T(4,128)S(1)}, u32[]{:S(2)}, u32[]{:S(2)}) collective-permute-start(f32[4,4,768]{2,1,0:T(4,128)} %norms.1.norm_ref), channel_id=1, source_target_pairs={{0,32},{32,64},{64,96},{96,0},{1,33},{33,65},{65,97},{97,1},{2,34}... | collective-permute-start | bytes 147464 | tf_op jit(solution)/shard_map/ppermute | solution.py:257
  92.3 9.3 %collective-permute-start.4 = (f32[4,4,768]{2,1,0:T(4,128)}, f32[4,4,768]{2,1,0:T(4,128)S(1)}, u32[]{:S(2)}, u32[]{:S(2)}) collective-permute-start(f32[4,4,768]{2,1,0:T(4,128)} %norms.1.norm_ref), channel_id=1, source_target_pairs={{0,64},{32,96},{64,0},{96,32},{1,65},{33,97},{65,1},{97,33},{2,66}... | collective-permute-start | bytes 147464 | tf_op jit(solution)/shard_map/ppermute | solution.py:257
  94.8 6.7 %collective-permute-start.3 = (f32[4,4,768]{2,1,0:T(4,128)}, f32[4,4,768]{2,1,0:T(4,128)S(1)}, u32[]{:S(2)}, u32[]{:S(2)}) collective-permute-start(f32[4,4,768]{2,1,0:T(4,128)} %norms.1.norm_ref), channel_id=1, source_target_pairs={{0,96},{32,0},{64,32},{96,64},{1,97},{33,1},{65,33},{97,65},{2,98}... | collective-permute-start | bytes 147464 | tf_op jit(solution)/shard_map/ppermute | solution.py:257
  101.6 0.6 copy-start.3
  101.6 0.6 copy-start.4
  101.6 0.6 copy-start.5

commit v4 on v3

--- a/solution.py
+++ b/solution.py
@@ -38,20 +38,23 @@
         out_ref[0, at:at + 128, (h % 2) * 128:(h % 2 + 1) * 128] = nt(rows, rows).astype(BF16)
 
 
-def partial_kernel(got_ref, out_ref):
-    for c in range(2):
-        acc = jnp.zeros((512, 256), F32)
-        for s in range(4):
-            acc += nn(got_ref[s, 512:1024, :], got_ref[s, c * 256:(c + 1) * 256, :])
-        out_ref[:, :, c * 256:(c + 1) * 256] = acc.reshape(8, 64, 256)
-    for pair in range(2):
-        gram = jnp.zeros((128, 256), F32)
-        for s in range(4):
-            gram += got_ref[s, 1024 + pair * 128:1024 + (pair + 1) * 128, :].astype(F32)
-        for k in range(2):
-            h = 2 * pair + k
-            out_ref[2 * h, :, 512:640] = gram[:64, k * 128:(k + 1) * 128]
-            out_ref[2 * h + 1, :, 512:640] = gram[64:, k * 128:(k + 1) * 128]
+def partial_kernel(got_ref, out_ref, buf, sems):
+    copies = [pltpu.make_async_copy(got_ref.at[s], buf.at[s], sems.at[s]) for s in range(4)]
+    for copy in copies:
+        copy.start()
+    for s in range(4):
+        copies[s].wait()
+        parts = [
+            nn(buf[s, 512:1024, :], buf[s, c * 256:(c + 1) * 256, :]).reshape(8, 64, 256)
+            for c in range(2)
+        ]
+        grams = []
+        for h in range(4):
+            at = 1024 + (h // 2) * 128
+            gram = buf[s, at:at + 128, (h % 2) * 128:(h % 2 + 1) * 128].astype(F32)
+            grams.append(gram.reshape(2, 64, 128))
+        part = jnp.concatenate(parts + [jnp.concatenate(grams, axis=0)], axis=2)
+        out_ref[...] = part if s == 0 else out_ref[...] + part
 
 
 def sum_kernel(got_ref, out_ref):
@@ -122,74 +125,88 @@
     return info_ref[0] + info_ref[1] * 32 + 3 * 128 + 31
 
 
-def score_tiles(info_ref, q_ref, keys, norms, p_ref, acc, tiles):
-    j = pl.program_id(0)
+def score_tiles(info_ref, block_ref, keys, norms, p_ref, buf, acc, sems, tiles):
     slab, me = info_ref[0], info_ref[1]
     at = lax.broadcasted_iota(jnp.int32, (128, 128), 1)
-
-    def scored(n, first, masked):
-        k = keys[n][...]
+    firsts = [tile_first(info_ref, s) for s in tiles]
+    unseen = [first > last_row(info_ref) for first in firsts]
+
+    def copy(j, n):
+        heads = pl.ds(4 * j, 4)
+        return pltpu.make_async_copy(buf.at[heads, n], p_ref.at[heads, n], sems.at[j, n])
+
+    def scored(j, n, masked):
+        k = keys[n][pl.ds(pl.multiple_of((j // 2) * 128, 128), 128), :]
         stat = acc[n]
         if masked:
             row = lax.broadcasted_iota(jnp.int32, (128, 1), 0)
             q_pos = slab + (row // 32) * 128 + me * 32 + row % 32
-            seen = lax.broadcasted_iota(jnp.int32, (128, 768), 1) <= q_pos - first
+            seen = lax.broadcasted_iota(jnp.int32, (128, 768), 1) <= q_pos - firsts[n]
         for i in range(4):
-            q = q_ref[:, 0, :, i * 128:(i + 1) * 128].reshape(128, 128)
+            q = block_ref[:, j, 0:16, i * 128:(i + 1) * 128].reshape(128, 128)
             scores = nn(q, k)
             if masked:
                 scores = jnp.where(seen, scores, MASKED)
             peak = jnp.max(scores, axis=1, keepdims=True) * SCALE
             e = jnp.exp2(scores * SCALE - peak)
-            p = e * norms[n][0, i:i + 1, :]
+            p = e * norms[n][j, i:i + 1, :]
             h = 4 * j + i
             stat = jnp.where(at == h, peak, stat)
             stat = jnp.where(at == h + 16, jnp.sum(e, axis=1, keepdims=True), stat)
             stat = jnp.where(at == h + 32, jnp.sum(p, axis=1, keepdims=True), stat)
-            p_ref[i, n] = p.astype(BF16)
+            buf[h, n] = p.astype(BF16)
         acc[n] = stat
-
-    for n, s in enumerate(tiles):
-        first = tile_first(info_ref, s)
-        full = first + 767 <= slab + me * 32
-        none = first > last_row(info_ref)
-
-        @pl.when(full)
-        def _():
-            scored(n, first, False)
-
-        @pl.when(jnp.logical_not(full) & jnp.logical_not(none))
-        def _():
-            scored(n, first, True)
-
-        @pl.when(none)
-        def _():
-            acc[n] = jnp.where(at < 16, MASKED, 0.0)
-
-
-def own_kernel(info_ref, q_ref, key_ref, norm_ref, p_ref, stat_ref, acc):
-    score_tiles(info_ref, q_ref, [key_ref], [norm_ref], p_ref, acc, (0,))
-
-    @pl.when(pl.program_id(0) == 3)
-    def _():
-        stat_ref[...] = acc[0].T[:48]
-
-
-def other_kernel(info_ref, q_ref, own_ref, *refs):
-    p_ref, stat_ref, peak_ref, acc = refs[6:]
-    score_tiles(info_ref, q_ref, refs[0:3], refs[3:6], p_ref, acc, (1, 2, 3))
-
-    @pl.when(pl.program_id(0) == 3)
-    def _():
-        stats = jnp.stack([own_ref[...]] + [acc[n].T[:48] for n in range(3)])
-        peaks = stats[:, 0:16]
-        peak = jnp.max(peaks, axis=0)
-        factor = jnp.exp2(peaks - peak[None])
-        denom = jnp.sum(stats[:, 16:32] * factor, axis=0)
-        part = jnp.sum(stats[:, 32:48] * factor, axis=0)
-        merged = jnp.concatenate([peak, denom, part], axis=0)
-        stat_ref[...] = jnp.broadcast_to(merged[None], (8, 48, 128))
-        peak_ref[...] = peaks
+        copy(j, n).start()
+
+    for n in range(len(tiles)):
+        acc[n] = jnp.where(at < 16, MASKED, 0.0)
+
+    def heads(j, carry):
+        for n in range(len(tiles)):
+            full = firsts[n] + 767 <= slab + me * 32
+
+            @pl.when(full)
+            def _():
+                scored(j, n, False)
+
+            @pl.when(jnp.logical_not(full) & jnp.logical_not(unseen[n]))
+            def _():
+                scored(j, n, True)
+        return carry
+
+    lax.fori_loop(0, 4, heads, 0)
+
+    def finish():
+        for n in range(len(tiles)):
+            @pl.when(jnp.logical_not(unseen[n]))
+            def _():
+                for j in range(4):
+                    copy(j, n).wait()
+
+    return finish
+
+
+def own_kernel(info_ref, block_ref, key_ref, norm_ref, p_ref, stat_ref, buf, acc, sems):
+    finish = score_tiles(info_ref, block_ref, [key_ref], [norm_ref], p_ref, buf, acc, sems, (0,))
+    stat_ref[...] = acc[0].T[:48]
+    finish()
+
+
+def other_kernel(info_ref, block_ref, own_ref, *refs):
+    p_ref, stat_ref, peak_ref, buf, acc, sems = refs[6:]
+    finish = score_tiles(
+        info_ref, block_ref, refs[0:3], refs[3:6], p_ref, buf, acc, sems, (1, 2, 3)
+    )
+    stats = jnp.stack([own_ref[...]] + [acc[n].T[:48] for n in range(3)])
+    peaks = stats[:, 0:16]
+    peak = jnp.max(peaks, axis=0)
+    factor = jnp.exp2(peaks - peak[None])
+    denom = jnp.sum(stats[:, 16:32] * factor, axis=0)
+    part = jnp.sum(stats[:, 32:48] * factor, axis=0)
+    merged = jnp.concatenate([peak, denom, part], axis=0)
+    stat_ref[...] = jnp.broadcast_to(merged[None], (8, 48, 128))
+    peak_ref[...] = peaks
+    finish()
 
 
 def map_kernel(info_ref, own_p_ref, p_ref, peak_ref, all_ref, out_ref, buf, w_scr, sems):
@@ -265,6 +282,7 @@
 
     params = pltpu.CompilerParams(vmem_limit_bytes=VMEM_LIMIT)
     vmem = pl.BlockSpec(memory_space=pltpu.VMEM)
+    smem, hbm = pl.BlockSpec(memory_space=pltpu.SMEM), pl.BlockSpec(memory_space=pl.ANY)
     pay = pl.pallas_call(
         pack_kernel,
         out_shape=jax.ShapeDtypeStruct((4, 1280, 256), BF16),
@@ -289,8 +307,9 @@
     parts = pl.pallas_call(
         partial_kernel,
         out_shape=jax.ShapeDtypeStruct((8, 64, 640), F32),
-        in_specs=[vmem],
+        in_specs=[hbm],
         out_specs=vmem,
+        scratch_shapes=[pltpu.VMEM((4, 1280, 256), BF16), pltpu.SemaphoreType.DMA((4,))],
         compiler_params=params,
         name="partial",
     )(got)
@@ -316,51 +335,33 @@
     )(own_values, block)
     norms = [norms] + from_others(norms)
 
-    q_spec = pl.BlockSpec((8, 1, 16, 512), lambda j, i: (0, j, 0, 0))
-    k_spec = pl.BlockSpec((128, 768), lambda j, i: (j // 2, 0))
-    n_spec = pl.BlockSpec((1, 4, 768), lambda j, i: (j, 0, 0))
-    stat_spec = pl.BlockSpec((48, 128), lambda j, i: (0, 0))
-    own_p, own_stats = pl.pallas_call(
-        own_kernel,
-        out_shape=(
-            jax.ShapeDtypeStruct((16, 1, 128, 768), BF16),
-            jax.ShapeDtypeStruct((48, 128), F32),
-        ),
-        grid_spec=pltpu.PrefetchScalarGridSpec(
-            num_scalar_prefetch=1,
-            grid=(4,),
-            in_specs=[q_spec, k_spec, n_spec],
-            out_specs=(pl.BlockSpec((4, 1, 128, 768), lambda j, i: (j, 0, 0, 0)), stat_spec),
-            scratch_shapes=[pltpu.VMEM((1, 128, 128), F32)],
-        ),
-        compiler_params=params,
-        name="own_scores",
-    )(info, block, keys[0], norms[0])
-    p, stats, peaks = pl.pallas_call(
-        other_kernel,
-        out_shape=(
-            jax.ShapeDtypeStruct((16, 3, 128, 768), BF16),
-            jax.ShapeDtypeStruct((8, 48, 128), F32),
-            jax.ShapeDtypeStruct((4, 16, 128), F32),
-        ),
-        grid_spec=pltpu.PrefetchScalarGridSpec(
-            num_scalar_prefetch=1,
-            grid=(4,),
-            in_specs=[q_spec, stat_spec] + [k_spec] * 3 + [n_spec] * 3,
-            out_specs=(
-                pl.BlockSpec((4, 3, 128, 768), lambda j, i: (j, 0, 0, 0)),
-                pl.BlockSpec((8, 48, 128), lambda j, i: (0, 0, 0)),
-                pl.BlockSpec((4, 16, 128), lambda j, i: (0, 0, 0)),
-            ),
-            scratch_shapes=[pltpu.VMEM((3, 128, 128), F32)],
-        ),
-        compiler_params=params,
-        name="scores",
-    )(info, block, own_stats, *keys[1:], *norms[1:])
+
+    def scores_call(kernel, count, name, shapes, *operands):
+        return pl.pallas_call(
+            kernel,
+            out_shape=[jax.ShapeDtypeStruct((16, count, 128, 768), BF16)]
+            + [jax.ShapeDtypeStruct(shape, F32) for shape in shapes],
+            in_specs=[smem] + [vmem] * len(operands),
+            out_specs=[hbm] + [vmem] * len(shapes),
+            scratch_shapes=[
+                pltpu.VMEM((16, count, 128, 768), BF16),
+                pltpu.VMEM((count, 128, 128), F32),
+                pltpu.SemaphoreType.DMA((4, count)),
+            ],
+            compiler_params=params,
+            name=name,
+        )(info, *operands)
+
+    own_p, own_stats = scores_call(
+        own_kernel, 1, "own_scores", [(48, 128)], block, keys[0], norms[0]
+    )
+    p, stats, peaks = scores_call(
+        other_kernel, 3, "scores", [(8, 48, 128), (4, 16, 128)],
+        block, own_stats, *keys[1:], *norms[1:],
+    )
 
     all_stats = lax.all_to_all(stats, ZY, 0, 0, tiled=True)
 
-    smem, hbm = pl.BlockSpec(memory_space=pltpu.SMEM), pl.BlockSpec(memory_space=pl.ANY)
     pay = pl.pallas_call(
         map_kernel,
         out_shape=jax.ShapeDtypeStruct((4, 128, 896), BF16),

time: 162 us -> 162 us (level)
  no operation moved by 1% of the time
where the time goes in v4:
time: 162 us; the launch traced here: 161 us
  blocking collectives  79.5 us (49%)
  Pallas kernels  58.4 us (36%)
  starting transfers between devices  12.8 us (8%)
  waiting for transfers between devices  7.31 us (5%)
  local copies, waits for them, and re-layouts  2.1 us (1%)
    all_to_all x1, blocking collectives, local(): got = lax.all_to_all(pay.reshape(16, 32, 896), MAP, 0, 0, tiled=True)  28.2 us
    all_to_all x1, blocking collectives, local(): parts = lax.all_to_all(parts, XZ, 0, 0, tiled=True)  21.1 us
    all_to_all x1, blocking collectives, local(): block = lax.all_to_all(block.reshape(32, 32, 512), CTX, 0, 0, tiled=True)  20.4 us
    pallas_call x2, Pallas kernels, scores_call(): pl.pallas_call(kernel, out_shape=[jax.ShapeDtypeStruct((16, count, 128, 7...  18.4 us
    pallas_call x2, Pallas kernels, project(): pl.pallas_call(project_kernel, out_shape=jax.ShapeDtypeStruct((256, 768),...  17.6 us
    all_to_all x1, blocking collectives, local(): all_stats = lax.all_to_all(stats, ZY, 0, 0, tiled=True)  9.8 us
    ppermute x6, starting transfers between devices, from_others(): lax.ppermute(array, 'x', [(i, (i - s) % NX) for i in range(NX)])  7.76 us
    pallas_call x1, Pallas kernels, local(): pl.pallas_call(map_kernel, out_shape=jax.ShapeDtypeStruct((4, 128, 896),...  7.39 us
  transfers between devices with their start and end apart: 7, of which 3 were waited for; matrix products, arithmetic and copies ran while one was open for 0% of the time, Pallas kernels for 15%

profile of v4, /device:TPU:1, one launch (start us, length us, event | category | flops | bytes accessed | tf_op | source)
XLA Modules:
  0.0 161.5 jit_solution(4396781790652400793)
XLA Ops:
  0.0 4.3 %pack.1 = bf16[4,1280,256]{2,1,0:T(8,128)(2,1)} custom-call(bf16[256,2048]{1,0:T(8,128)(2,1)} %wq_ref.1, bf16[512,256]{1,0:T(8,128)(2,1)} %qs_ref.1, bf16[2048,256]{1,0:T(8,128)(2,1)} %wo_ref.1), custom_call_target="tpu_custom_call" | custom-call | tf_op jit(solution)/shard_map/pack/pallas_call | solution.py:286
  4.3 5.0 %all-to-all-start = ((bf16[4,1280,256]{2,1,0:T(8,128)(2,1)}), bf16[4,1280,256]{2,1,0:T(8,128)(2,1)S(1)}, u32[]{:S(2)}, u32[]{:S(2)}) async-start(bf16[4,1280,256]{2,1,0:T(8,128)(2,1)} %pack.1), calls=%async_computation | async-start | bytes 5242880 | tf_op jit(solution)/shard_map/all_to_all | solution.py:299
  9.4 8.8 %project_keys.1.key_ref = bf16[256,768]{1,0:T(8,128)(2,1)} custom-call(bf16[768,8192]{1,0:T(8,128)(2,1)} %state_ref.3, bf16[8192,256]{1,0:T(8,128)(2,1)} %w_ref.3), custom_call_target="tpu_custom_call" | custom-call | tf_op jit(solution)/shard_map/project_keys/pallas_call | solution.py:90
  18.2 1.2 collective-permute-start.2
  19.4 2.5 %collective-permute-start.1 = (bf16[256,768]{1,0:T(8,128)(2,1)}, bf16[256,768]{1,0:T(8,128)(2,1)S(1)}, u32[]{:S(2)}, u32[]{:S(2)}) collective-permute-start(bf16[256,768]{1,0:T(8,128)(2,1)} %project_keys.1.key_ref), channel_id=1, source_target_pairs={{0,64},{32,96},{64,0},{96,32},{1,65},{33,97},{65,1},{97,33},{2,66}... | collective-permute-start | bytes 1179656 | tf_op jit(solution)/shard_map/ppermute | solution.py:274
  21.8 1.2 collective-permute-start
  23.6 8.8 %project_values.1.value_ref = bf16[256,768]{1,0:T(8,128)(2,1)} custom-call(bf16[768,8192]{1,0:T(8,128)(2,1)} %state_ref.3, bf16[8192,256]{1,0:T(8,128)(2,1)} %w_ref.2), custom_call_target="tpu_custom_call" | custom-call | tf_op jit(solution)/shard_map/project_values/pallas_call | solution.py:90
  32.5 0.6 pad_add_fusion.info_ref
  33.1 0.0 collective-permute-done.2.refs_2_
  33.1 5.6 %collective-permute-done.1.refs_1_ = bf16[256,768]{1,0:T(8,128)(2,1)S(1)} collective-permute-done((bf16[256,768]{1,0:T(8,128)(2,1)}, bf16[256,768]{1,0:T(8,128)(2,1)S(1)}, u32[]{:S(2)}, u32[]{:S(2)}) %collective-permute-start.1) | collective-permute-done | bytes 393248 | tf_op jit(solution)/shard_map/ppermute | solution.py:274
  38.7 0.1 collective-permute-done.refs_0_
  38.7 1.7 %all-to-all-done.got_ref = bf16[4,1280,256]{2,1,0:T(8,128)(2,1)S(1)} async-done(((bf16[4,1280,256]{2,1,0:T(8,128)(2,1)}), bf16[4,1280,256]{2,1,0:T(8,128)(2,1)S(1)}, u32[]{:S(2)}, u32[]{:S(2)}) %all-to-all-start) | async-done | bytes 2621472 | tf_op jit(solution)/shard_map/all_to_all | solution.py:299
  40.4 1.5 copy-done
  41.9 3.1 %partial.1 = f32[8,64,640]{2,1,0:T(8,128)} custom-call(bf16[4,1280,256]{2,1,0:T(8,128)(2,1)} %copy-done), custom_call_target="tpu_custom_call" | custom-call | tf_op jit(solution)/shard_map/partial/pallas_call | solution.py:307
  45.0 21.1 %all_to_all.25.got_ref = f32[8,64,640]{2,1,0:T(8,128)} all-to-all(f32[8,64,640]{2,1,0:T(8,128)} %partial.1), channel_id=1, replica_groups=mesh['x'=4,'zl'=2,'y'=4,'zh'=2,'core'=2] {'x','zl'}, dimensions={0} | all-to-all | bytes 2621440 | tf_op jit(solution)/shard_map/all_to_all | solution.py:316
  66.1 2.4 %sum.1 = bf16[4,8,32,512]{3,2,1,0:T(8,128)(2,1)} custom-call(f32[8,64,640]{2,1,0:T(8,128)} %all_to_all.25.got_ref), custom_call_target="tpu_custom_call" | custom-call | tf_op jit(solution)/shard_map/sum/pallas_call | solution.py:317
  68.5 20.4 %all_to_all.26 = bf16[32,32,512]{2,1,0:T(8,128)(2,1)} all-to-all(bf16[32,32,512]{2,1,0:T(8,128)(2,1)} %bitcast.9), channel_id=1, replica_groups=mesh['x'=4,'zl'=2,'y'=4,'zh'=2,'core'=2] {'x','zl','y'}, dimensions={0} | all-to-all | bytes 2097152 | tf_op jit(solution)/shard_map/all_to_all | solution.py:325
  88.9 3.0 %norms.1.norm_ref = f32[4,4,768]{2,1,0:T(4,128)} custom-call(bf16[256,768]{1,0:T(8,128)(2,1)} %project_values.1.value_ref, bf16[8,4,32,512]{3,2,1,0:T(8,128)(2,1)} %bitcast.6), custom_call_target="tpu_custom_call" | custom-call | tf_op jit(solution)/shard_map/norms/pallas_call | solution.py:328
  91.9 0.0 collective-permute-start.5
  91.9 2.5 %collective-permute-start.4 = (f32[4,4,768]{2,1,0:T(4,128)}, f32[4,4,768]{2,1,0:T(4,128)S(1)}, u32[]{:S(2)}, u32[]{:S(2)}) collective-permute-start(f32[4,4,768]{2,1,0:T(4,128)} %norms.1.norm_ref), channel_id=1, source_target_pairs={{0,64},{32,96},{64,0},{96,32},{1,65},{33,97},{65,1},{97,33},{2,66}... | collective-permute-start | bytes 147464 | tf_op jit(solution)/shard_map/ppermute | solution.py:274
  94.5 0.4 collective-permute-start.3
  94.9 5.9 %own_scores.1 = (bf16[16,1,128,768]{3,2,1,0:T(8,128)(2,1)}, f32[48,128]{1,0:T(8,128)}) custom-call(s32[4]{0:T(128)} %pad_add_fusion.info_ref, bf16[8,4,32,512]{3,2,1,0:T(8,128)(2,1)} %bitcast.7, bf16[256,768]{1,0:T(8,128)(2,1)} %project_keys.1.key_ref, f32[4,4,768]{2,1,0:T(4,128)} %norms.1.norm_ref), custom_call_target="tpu_custom_call" | custom-call | tf_op jit(solution)/shard_map/own_scores/pallas_call | solution.py:340
  100.8 0.0 collective-permute-done.5.refs_5_
  100.8 0.0 collective-permute-done.4.refs_4_
  100.9 0.6 copy-done.3
  101.4 0.0 copy-done.4
  101.4 0.0 copy-done.5
  101.5 12.5 %scores.1 = (bf16[16,3,128,768]{3,2,1,0:T(8,128)(2,1)}, f32[8,48,128]{2,1,0:T(8,128)}, f32[4,16,128]{2,1,0:T(8,128)}) custom-call(s32[4]{0:T(128)} %pad_add_fusion.info_ref, bf16[8,4,32,512]{3,2,1,0:T(8,128)(2,1)} %bitcast.8, f32[48,128]{1,0:T(8,128)} %get-tuple-element.20.own_ref, bf16[256,768]{1,0:T(8,128)(2,1)} %collective-permute-done.refs_0_, ...), custom_call_target="tpu_custom_call" | custom-call | tf_op jit(solution)/shard_map/scores/pallas_call | solution.py:340
  114.0 9.8 %all_to_all.27.all_ref = f32[8,48,128]{2,1,0:T(8,128)} all-to-all(f32[8,48,128]{2,1,0:T(8,128)} %get-tuple-element.26), channel_id=1, replica_groups=mesh['x'=4,'zl'=2,'y'=4,'zh'=2,'core'=2] {'zl','y'}, dimensions={0} | all-to-all | bytes 393216 | tf_op jit(solution)/shard_map/all_to_all | solution.py:363
  123.8 7.4 %weigh.1 = bf16[4,128,896]{2,1,0:T(8,128)(2,1)} custom-call(s32[4]{0:T(128)} %pad_add_fusion.info_ref, bf16[16,1,128,768]{3,2,1,0:T(8,128)(2,1)} %get-tuple-element.19.own_p_ref, bf16[16,3,128,768]{3,2,1,0:T(8,128)(2,1)} %get-tuple-element.24.p_ref, f32[4,16,128]{2,1,0:T(8,128)} %get-tuple-element.25.peak_ref, f32[8,48,128]{2,1,0:T(8,128)} %all_to_all.27.all_ref), custom_call_target="tpu_custom_call" | custom-call | tf_op jit(solution)/shard_map/weigh/pallas_call | solution.py:365
  131.2 28.2 %all_to_all.28.got_ref = bf16[16,32,896]{2,1,0:T(8,128)(2,1)} all-to-all(bf16[16,32,896]{2,1,0:T(8,128)(2,1)} %bitcast.10), channel_id=1, replica_groups=mesh['x'=4,'zl'=2,'y'=4,'zh'=2,'core'=2] {'x','zh','core'}, dimensions={0} | all-to-all | bytes 1835008 | tf_op jit(solution)/shard_map/all_to_all | solution.py:378
  159.4 2.1 %finish.1 = f32[128,768]{1,0:T(8,128)} custom-call(s32[4]{0:T(128)} %pad_add_fusion.info_ref, bf16[16,32,896]{2,1,0:T(8,128)(2,1)} %all_to_all.28.got_ref), custom_call_target="tpu_custom_call" | custom-call | tf_op jit(solution)/shard_map/finish/pallas_call | solution.py:380
  (9 shorter events, 0.0 us)
Async XLA Ops:
  4.3 36.1 %all-to-all-start = ((bf16[4,1280,256]{2,1,0:T(8,128)(2,1)}), bf16[4,1280,256]{2,1,0:T(8,128)(2,1)S(1)}, u32[]{:S(2)}, u32[]{:S(2)}) async-start(bf16[4,1280,256]{2,1,0:T(8,128)(2,1)} %pack.1), calls=%async_computation | async-start | bytes 5242880 | tf_op jit(solution)/shard_map/all_to_all | solution.py:299
  18.2 14.9 %collective-permute-start.2 = (bf16[256,768]{1,0:T(8,128)(2,1)}, bf16[256,768]{1,0:T(8,128)(2,1)S(1)}, u32[]{:S(2)}, u32[]{:S(2)}) collective-permute-start(bf16[256,768]{1,0:T(8,128)(2,1)} %project_keys.1.key_ref), channel_id=1, source_target_pairs={{0,32},{32,64},{64,96},{96,0},{1,33},{33,65},{65,97},{97,1},{2,34}... | collective-permute-start | bytes 1179656 | tf_op jit(solution)/shard_map/ppermute | solution.py:274
  19.4 19.3 %collective-permute-start.1 = (bf16[256,768]{1,0:T(8,128)(2,1)}, bf16[256,768]{1,0:T(8,128)(2,1)S(1)}, u32[]{:S(2)}, u32[]{:S(2)}) collective-permute-start(bf16[256,768]{1,0:T(8,128)(2,1)} %project_keys.1.key_ref), channel_id=1, source_target_pairs={{0,64},{32,96},{64,0},{96,32},{1,65},{33,97},{65,1},{97,33},{2,66}... | collective-permute-start | bytes 1179656 | tf_op jit(solution)/shard_map/ppermute | solution.py:274
  21.8 16.9 %collective-permute-start = (bf16[256,768]{1,0:T(8,128)(2,1)}, bf16[256,768]{1,0:T(8,128)(2,1)}, u32[]{:S(2)}, u32[]{:S(2)}) collective-permute-start(bf16[256,768]{1,0:T(8,128)(2,1)} %project_keys.1.key_ref), channel_id=1, source_target_pairs={{0,96},{32,0},{64,32},{96,64},{1,97},{33,1},{65,33},{97,65},{2,98}... | collective-permute-start | bytes 1179656 | tf_op jit(solution)/shard_map/ppermute | solution.py:274
  33.1 67.8 %copy-start.1 = (bf16[256,768]{1,0:T(8,128)(2,1)}, bf16[256,768]{1,0:T(8,128)(2,1)S(1)}, u32[]{:S(2)}) copy-start(bf16[256,768]{1,0:T(8,128)(2,1)S(1)} %collective-permute-done.2.refs_2_) | copy-start | bytes 1179652
  38.7 62.2 %copy-start.2 = (bf16[256,768]{1,0:T(8,128)(2,1)}, bf16[256,768]{1,0:T(8,128)(2,1)S(1)}, u32[]{:S(2)}) copy-start(bf16[256,768]{1,0:T(8,128)(2,1)S(1)} %collective-permute-done.1.refs_1_) | copy-start | bytes 1179652
  40.4 1.5 copy-start
  91.9 8.9 %collective-permute-start.5 = (f32[4,4,768]{2,1,0:T(4,128)}, f32[4,4,768]{2,1,0:T(4,128)S(1)}, u32[]{:S(2)}, u32[]{:S(2)}) collective-permute-start(f32[4,4,768]{2,1,0:T(4,128)} %norms.1.norm_ref), channel_id=1, source_target_pairs={{0,32},{32,64},{64,96},{96,0},{1,33},{33,65},{65,97},{97,1},{2,34}... | collective-permute-start | bytes 147464 | tf_op jit(solution)/shard_map/ppermute | solution.py:274
  91.9 8.9 %collective-permute-start.4 = (f32[4,4,768]{2,1,0:T(4,128)}, f32[4,4,768]{2,1,0:T(4,128)S(1)}, u32[]{:S(2)}, u32[]{:S(2)}) collective-permute-start(f32[4,4,768]{2,1,0:T(4,128)} %norms.1.norm_ref), channel_id=1, source_target_pairs={{0,64},{32,96},{64,0},{96,32},{1,65},{33,97},{65,1},{97,33},{2,66}... | collective-permute-start | bytes 147464 | tf_op jit(solution)/shard_map/ppermute | solution.py:274
  94.5 6.4 %collective-permute-start.3 = (f32[4,4,768]{2,1,0:T(4,128)}, f32[4,4,768]{2,1,0:T(4,128)S(1)}, u32[]{:S(2)}, u32[]{:S(2)}) collective-permute-start(f32[4,4,768]{2,1,0:T(4,128)} %norms.1.norm_ref), channel_id=1, source_target_pairs={{0,96},{32,0},{64,32},{96,64},{1,97},{33,1},{65,33},{97,65},{2,98}... | collective-permute-start | bytes 147464 | tf_op jit(solution)/shard_map/ppermute | solution.py:274
  100.8 0.6 copy-start.3
  100.8 0.6 copy-start.4
  100.8 0.6 copy-start.5

commit v5 on v4

--- a/solution.py
+++ b/solution.py
@@ -23,19 +23,43 @@
     return lax.dot_general(a, b, (((1,), (1,)), ((), ())), preferred_element_type=F32)
 
 
-def pack_kernel(wq_ref, qs_ref, wo_ref, out_ref):
-    out_ref[0, 0:256, :] = wq_ref[:, 0:256]
-    out_ref[0, 256:512, :] = wq_ref[:, 256:512]
-    for block in range(4):
-        for part in range(4):
-            for half in range(2):
-                src = ((block * 4 + part) * 2 + half) * 16
-                dst = 512 + ((block * 2 + half) * 4 + part) * 16
-                out_ref[0, dst:dst + 16, :] = qs_ref[src:src + 16, :]
-    for h in range(4):
-        rows = wo_ref[h * 128:(h + 1) * 128, :]
-        at = 1024 + (h // 2) * 128
-        out_ref[0, at:at + 128, (h % 2) * 128:(h % 2 + 1) * 128] = nt(rows, rows).astype(BF16)
+def pack_kernel(wq_ref, qs_ref, wo_ref, out_ref, buf, qs_buf, wo_buf, qs_sem, wq_sems, wo_sems, sems):
+    rows_in = pltpu.make_async_copy(qs_ref, qs_buf, qs_sem)
+    rows_in.start()
+    columns_in, heads_in = [], []
+    for i in range(4):
+        heads_in.append(
+            pltpu.make_async_copy(wo_ref.at[pl.ds(i * 512, 512)], wo_buf.at[i], wo_sems.at[i])
+        )
+        heads_in[i].start()
+        for c in range(2):
+            copy = pltpu.make_async_copy(
+                wq_ref.at[:, pl.ds((2 * i + c) * 256, 256)],
+                buf.at[i, pl.ds(c * 256, 256)],
+                wq_sems.at[i, c],
+            )
+            copy.start()
+            columns_in.append(copy)
+    rows_in.wait()
+    copies_out = []
+    for i in range(4):
+        for block in range(4):
+            for part in range(4):
+                for half in range(2):
+                    src = ((block * 4 + part) * 2 + half) * 16
+                    dst = 512 + ((block * 2 + half) * 4 + part) * 16
+                    buf[i, dst:dst + 16, :] = qs_buf[src:src + 16, :]
+        heads_in[i].wait()
+        for h in range(4):
+            rows = wo_buf[i, h * 128:(h + 1) * 128, :]
+            at = 1024 + (h // 2) * 128
+            buf[i, at:at + 128, (h % 2) * 128:(h % 2 + 1) * 128] = nt(rows, rows).astype(BF16)
+        columns_in[2 * i].wait()
+        columns_in[2 * i + 1].wait()
+        copies_out.append(pltpu.make_async_copy(buf.at[i], out_ref.at[i], sems.at[i]))
+        copies_out[i].start()
+    for copy in copies_out:
+        copy.wait()
 
 
 def partial_kernel(got_ref, out_ref, buf, sems):
@@ -286,13 +310,17 @@
     pay = pl.pallas_call(
         pack_kernel,
         out_shape=jax.ShapeDtypeStruct((4, 1280, 256), BF16),
-        grid=(4,),
-        in_specs=[
-            pl.BlockSpec((256, 512), lambda i: (0, i)),
-            pl.BlockSpec((512, 256), lambda i: (0, 0)),
-            pl.BlockSpec((512, 256), lambda i: (i, 0)),
+        in_specs=[hbm] * 3,
+        out_specs=hbm,
+        scratch_shapes=[
+            pltpu.VMEM((4, 1280, 256), BF16),
+            pltpu.VMEM((512, 256), BF16),
+            pltpu.VMEM((4, 512, 256), BF16),
+            pltpu.SemaphoreType.DMA,
+            pltpu.SemaphoreType.DMA((4, 2)),
+            pltpu.SemaphoreType.DMA((4,)),
+            pltpu.SemaphoreType.DMA((4,)),
         ],
-        out_specs=pl.BlockSpec((1, 1280, 256), lambda i: (i, 0, 0)),
         compiler_params=params,
         name="pack",
     )(w_query, query_states, w_out)

time: 162 us -> 160 us (0.988)
  no operation moved by 1% of the time
where the time goes in v5:
time: 160 us; the launch traced here: 161 us
  blocking collectives  79.6 us (50%)
  Pallas kernels  57.6 us (36%)
  starting transfers between devices  12.8 us (8%)
  waiting for transfers between devices  7.3 us (5%)
  local copies, waits for them, and re-layouts  2.1 us (1%)
    all_to_all x1, blocking collectives, local(): got = lax.all_to_all(pay.reshape(16, 32, 896), MAP, 0, 0, tiled=True)  27.6 us
    all_to_all x1, blocking collectives, local(): parts = lax.all_to_all(parts, XZ, 0, 0, tiled=True)  21.1 us
    all_to_all x1, blocking collectives, local(): block = lax.all_to_all(block.reshape(32, 32, 512), CTX, 0, 0, tiled=True)  20.4 us
    pallas_call x2, Pallas kernels, scores_call(): pl.pallas_call(kernel, out_shape=[jax.ShapeDtypeStruct((16, count, 128, 7...  18.4 us
    pallas_call x2, Pallas kernels, project(): pl.pallas_call(project_kernel, out_shape=jax.ShapeDtypeStruct((256, 768),...  17.6 us
    all_to_all x1, blocking collectives, local(): all_stats = lax.all_to_all(stats, ZY, 0, 0, tiled=True)  10.5 us
    ppermute x6, starting transfers between devices, from_others(): lax.ppermute(array, 'x', [(i, (i - s) % NX) for i in range(NX)])  7.76 us
    pallas_call x1, Pallas kernels, local(): pl.pallas_call(map_kernel, out_shape=jax.ShapeDtypeStruct((4, 128, 896),...  7.39 us
  transfers between devices with their start and end apart: 7, of which 3 were waited for; matrix products, arithmetic and copies ran while one was open for 0% of the time, Pallas kernels for 15%

profile of v5, /device:TPU:1, one launch (start us, length us, event | category | flops | bytes accessed | tf_op | source)
XLA Modules:
  0.0 160.8 jit_solution(15385595038353733049)
XLA Ops:
  0.0 3.6 %pack.1 = bf16[4,1280,256]{2,1,0:T(8,128)(2,1)} custom-call(bf16[256,2048]{1,0:T(8,128)(2,1)} %wq_ref.1, bf16[512,256]{1,0:T(8,128)(2,1)} %qs_ref.1, bf16[2048,256]{1,0:T(8,128)(2,1)} %wo_ref.1), custom_call_target="tpu_custom_call" | custom-call | tf_op jit(solution)/shard_map/pack/pallas_call | solution.py:310
  3.6 5.0 %all-to-all-start = ((bf16[4,1280,256]{2,1,0:T(8,128)(2,1)}), bf16[4,1280,256]{2,1,0:T(8,128)(2,1)S(1)}, u32[]{:S(2)}, u32[]{:S(2)}) async-start(bf16[4,1280,256]{2,1,0:T(8,128)(2,1)} %pack.1), calls=%async_computation | async-start | bytes 5242880 | tf_op jit(solution)/shard_map/all_to_all | solution.py:327
  8.6 8.8 %project_keys.1.key_ref = bf16[256,768]{1,0:T(8,128)(2,1)} custom-call(bf16[768,8192]{1,0:T(8,128)(2,1)} %state_ref.3, bf16[8192,256]{1,0:T(8,128)(2,1)} %w_ref.3), custom_call_target="tpu_custom_call" | custom-call | tf_op jit(solution)/shard_map/project_keys/pallas_call | solution.py:114
  17.4 1.2 collective-permute-start.2
  18.6 2.5 %collective-permute-start.1 = (bf16[256,768]{1,0:T(8,128)(2,1)}, bf16[256,768]{1,0:T(8,128)(2,1)S(1)}, u32[]{:S(2)}, u32[]{:S(2)}) collective-permute-start(bf16[256,768]{1,0:T(8,128)(2,1)} %project_keys.1.key_ref), channel_id=1, source_target_pairs={{0,64},{32,96},{64,0},{96,32},{1,65},{33,97},{65,1},{97,33},{2,66}... | collective-permute-start | bytes 1179656 | tf_op jit(solution)/shard_map/ppermute | solution.py:298
  21.1 1.1 collective-permute-start
  22.9 8.8 %project_values.1.value_ref = bf16[256,768]{1,0:T(8,128)(2,1)} custom-call(bf16[768,8192]{1,0:T(8,128)(2,1)} %state_ref.3, bf16[8192,256]{1,0:T(8,128)(2,1)} %w_ref.2), custom_call_target="tpu_custom_call" | custom-call | tf_op jit(solution)/shard_map/project_values/pallas_call | solution.py:114
  31.7 0.6 pad_add_fusion.info_ref
  32.4 0.0 collective-permute-done.2.refs_2_
  32.4 5.6 %collective-permute-done.1.refs_1_ = bf16[256,768]{1,0:T(8,128)(2,1)S(1)} collective-permute-done((bf16[256,768]{1,0:T(8,128)(2,1)}, bf16[256,768]{1,0:T(8,128)(2,1)S(1)}, u32[]{:S(2)}, u32[]{:S(2)}) %collective-permute-start.1) | collective-permute-done | bytes 393248 | tf_op jit(solution)/shard_map/ppermute | solution.py:298
  37.9 0.1 collective-permute-done.refs_0_
  38.0 1.7 %all-to-all-done.got_ref = bf16[4,1280,256]{2,1,0:T(8,128)(2,1)S(1)} async-done(((bf16[4,1280,256]{2,1,0:T(8,128)(2,1)}), bf16[4,1280,256]{2,1,0:T(8,128)(2,1)S(1)}, u32[]{:S(2)}, u32[]{:S(2)}) %all-to-all-start) | async-done | bytes 2621472 | tf_op jit(solution)/shard_map/all_to_all | solution.py:327
  39.7 1.5 copy-done
  41.2 3.1 %partial.1 = f32[8,64,640]{2,1,0:T(8,128)} custom-call(bf16[4,1280,256]{2,1,0:T(8,128)(2,1)} %copy-done), custom_call_target="tpu_custom_call" | custom-call | tf_op jit(solution)/shard_map/partial/pallas_call | solution.py:335
  44.3 21.1 %all_to_all.25.got_ref = f32[8,64,640]{2,1,0:T(8,128)} all-to-all(f32[8,64,640]{2,1,0:T(8,128)} %partial.1), channel_id=1, replica_groups=mesh['x'=4,'zl'=2,'y'=4,'zh'=2,'core'=2] {'x','zl'}, dimensions={0} | all-to-all | bytes 2621440 | tf_op jit(solution)/shard_map/all_to_all | solution.py:344
  65.4 2.4 %sum.1 = bf16[4,8,32,512]{3,2,1,0:T(8,128)(2,1)} custom-call(f32[8,64,640]{2,1,0:T(8,128)} %all_to_all.25.got_ref), custom_call_target="tpu_custom_call" | custom-call | tf_op jit(solution)/shard_map/sum/pallas_call | solution.py:345
  67.8 20.4 %all_to_all.26 = bf16[32,32,512]{2,1,0:T(8,128)(2,1)} all-to-all(bf16[32,32,512]{2,1,0:T(8,128)(2,1)} %bitcast.9), channel_id=1, replica_groups=mesh['x'=4,'zl'=2,'y'=4,'zh'=2,'core'=2] {'x','zl','y'}, dimensions={0} | all-to-all | bytes 2097152 | tf_op jit(solution)/shard_map/all_to_all | solution.py:353
  88.2 3.0 %norms.1.norm_ref = f32[4,4,768]{2,1,0:T(4,128)} custom-call(bf16[256,768]{1,0:T(8,128)(2,1)} %project_values.1.value_ref, bf16[8,4,32,512]{3,2,1,0:T(8,128)(2,1)} %bitcast.6), custom_call_target="tpu_custom_call" | custom-call | tf_op jit(solution)/shard_map/norms/pallas_call | solution.py:356
  91.2 0.0 collective-permute-start.5
  91.2 2.5 %collective-permute-start.4 = (f32[4,4,768]{2,1,0:T(4,128)}, f32[4,4,768]{2,1,0:T(4,128)S(1)}, u32[]{:S(2)}, u32[]{:S(2)}) collective-permute-start(f32[4,4,768]{2,1,0:T(4,128)} %norms.1.norm_ref), channel_id=1, source_target_pairs={{0,64},{32,96},{64,0},{96,32},{1,65},{33,97},{65,1},{97,33},{2,66}... | collective-permute-start | bytes 147464 | tf_op jit(solution)/shard_map/ppermute | solution.py:298
  93.7 0.4 collective-permute-start.3
  94.1 5.9 %own_scores.1 = (bf16[16,1,128,768]{3,2,1,0:T(8,128)(2,1)}, f32[48,128]{1,0:T(8,128)}) custom-call(s32[4]{0:T(128)} %pad_add_fusion.info_ref, bf16[8,4,32,512]{3,2,1,0:T(8,128)(2,1)} %bitcast.7, bf16[256,768]{1,0:T(8,128)(2,1)} %project_keys.1.key_ref, f32[4,4,768]{2,1,0:T(4,128)} %norms.1.norm_ref), custom_call_target="tpu_custom_call" | custom-call | tf_op jit(solution)/shard_map/own_scores/pallas_call | solution.py:368
  100.0 0.0 collective-permute-done.5.refs_5_
  100.1 0.0 collective-permute-done.3.refs_3_
  100.1 0.6 copy-done.3
  100.7 0.0 copy-done.4
  100.7 0.0 copy-done.5
  100.7 12.5 %scores.1 = (bf16[16,3,128,768]{3,2,1,0:T(8,128)(2,1)}, f32[8,48,128]{2,1,0:T(8,128)}, f32[4,16,128]{2,1,0:T(8,128)}) custom-call(s32[4]{0:T(128)} %pad_add_fusion.info_ref, bf16[8,4,32,512]{3,2,1,0:T(8,128)(2,1)} %bitcast.8, f32[48,128]{1,0:T(8,128)} %get-tuple-element.20.own_ref, bf16[256,768]{1,0:T(8,128)(2,1)} %collective-permute-done.refs_0_, ...), custom_call_target="tpu_custom_call" | custom-call | tf_op jit(solution)/shard_map/scores/pallas_call | solution.py:368
  113.2 10.5 %all_to_all.27.all_ref = f32[8,48,128]{2,1,0:T(8,128)} all-to-all(f32[8,48,128]{2,1,0:T(8,128)} %get-tuple-element.26), channel_id=1, replica_groups=mesh['x'=4,'zl'=2,'y'=4,'zh'=2,'core'=2] {'zl','y'}, dimensions={0} | all-to-all | bytes 393216 | tf_op jit(solution)/shard_map/all_to_all | solution.py:391
  123.7 7.4 %weigh.1 = bf16[4,128,896]{2,1,0:T(8,128)(2,1)} custom-call(s32[4]{0:T(128)} %pad_add_fusion.info_ref, bf16[16,1,128,768]{3,2,1,0:T(8,128)(2,1)} %get-tuple-element.19.own_p_ref, bf16[16,3,128,768]{3,2,1,0:T(8,128)(2,1)} %get-tuple-element.24.p_ref, f32[4,16,128]{2,1,0:T(8,128)} %get-tuple-element.25.peak_ref, f32[8,48,128]{2,1,0:T(8,128)} %all_to_all.27.all_ref), custom_call_target="tpu_custom_call" | custom-call | tf_op jit(solution)/shard_map/weigh/pallas_call | solution.py:393
  131.1 27.6 %all_to_all.28.got_ref = bf16[16,32,896]{2,1,0:T(8,128)(2,1)} all-to-all(bf16[16,32,896]{2,1,0:T(8,128)(2,1)} %bitcast.10), channel_id=1, replica_groups=mesh['x'=4,'zl'=2,'y'=4,'zh'=2,'core'=2] {'x','zh','core'}, dimensions={0} | all-to-all | bytes 1835008 | tf_op jit(solution)/shard_map/all_to_all | solution.py:406
  158.6 2.1 %finish.1 = f32[128,768]{1,0:T(8,128)} custom-call(s32[4]{0:T(128)} %pad_add_fusion.info_ref, bf16[16,32,896]{2,1,0:T(8,128)(2,1)} %all_to_all.28.got_ref), custom_call_target="tpu_custom_call" | custom-call | tf_op jit(solution)/shard_map/finish/pallas_call | solution.py:408
  (9 shorter events, 0.0 us)
Async XLA Ops:
  3.6 36.1 %all-to-all-start = ((bf16[4,1280,256]{2,1,0:T(8,128)(2,1)}), bf16[4,1280,256]{2,1,0:T(8,128)(2,1)S(1)}, u32[]{:S(2)}, u32[]{:S(2)}) async-start(bf16[4,1280,256]{2,1,0:T(8,128)(2,1)} %pack.1), calls=%async_computation | async-start | bytes 5242880 | tf_op jit(solution)/shard_map/all_to_all | solution.py:327
  17.4 14.9 %collective-permute-start.2 = (bf16[256,768]{1,0:T(8,128)(2,1)}, bf16[256,768]{1,0:T(8,128)(2,1)S(1)}, u32[]{:S(2)}, u32[]{:S(2)}) collective-permute-start(bf16[256,768]{1,0:T(8,128)(2,1)} %project_keys.1.key_ref), channel_id=1, source_target_pairs={{0,32},{32,64},{64,96},{96,0},{1,33},{33,65},{65,97},{97,1},{2,34}... | collective-permute-start | bytes 1179656 | tf_op jit(solution)/shard_map/ppermute | solution.py:298
  18.6 19.3 %collective-permute-start.1 = (bf16[256,768]{1,0:T(8,128)(2,1)}, bf16[256,768]{1,0:T(8,128)(2,1)S(1)}, u32[]{:S(2)}, u32[]{:S(2)}) collective-permute-start(bf16[256,768]{1,0:T(8,128)(2,1)} %project_keys.1.key_ref), channel_id=1, source_target_pairs={{0,64},{32,96},{64,0},{96,32},{1,65},{33,97},{65,1},{97,33},{2,66}... | collective-permute-start | bytes 1179656 | tf_op jit(solution)/shard_map/ppermute | solution.py:298
  21.1 16.9 %collective-permute-start = (bf16[256,768]{1,0:T(8,128)(2,1)}, bf16[256,768]{1,0:T(8,128)(2,1)}, u32[]{:S(2)}, u32[]{:S(2)}) collective-permute-start(bf16[256,768]{1,0:T(8,128)(2,1)} %project_keys.1.key_ref), channel_id=1, source_target_pairs={{0,96},{32,0},{64,32},{96,64},{1,97},{33,1},{65,33},{97,65},{2,98}... | collective-permute-start | bytes 1179656 | tf_op jit(solution)/shard_map/ppermute | solution.py:298
  32.4 67.7 %copy-start.1 = (bf16[256,768]{1,0:T(8,128)(2,1)}, bf16[256,768]{1,0:T(8,128)(2,1)S(1)}, u32[]{:S(2)}) copy-start(bf16[256,768]{1,0:T(8,128)(2,1)S(1)} %collective-permute-done.2.refs_2_) | copy-start | bytes 1179652
  37.9 62.2 %copy-start.2 = (bf16[256,768]{1,0:T(8,128)(2,1)}, bf16[256,768]{1,0:T(8,128)(2,1)S(1)}, u32[]{:S(2)}) copy-start(bf16[256,768]{1,0:T(8,128)(2,1)S(1)} %collective-permute-done.1.refs_1_) | copy-start | bytes 1179652
  39.7 1.5 copy-start
  91.2 8.9 %collective-permute-start.5 = (f32[4,4,768]{2,1,0:T(4,128)}, f32[4,4,768]{2,1,0:T(4,128)S(1)}, u32[]{:S(2)}, u32[]{:S(2)}) collective-permute-start(f32[4,4,768]{2,1,0:T(4,128)} %norms.1.norm_ref), channel_id=1, source_target_pairs={{0,32},{32,64},{64,96},{96,0},{1,33},{33,65},{65,97},{97,1},{2,34}... | collective-permute-start | bytes 147464 | tf_op jit(solution)/shard_map/ppermute | solution.py:298
  91.2 8.9 %collective-permute-start.4 = (f32[4,4,768]{2,1,0:T(4,128)}, f32[4,4,768]{2,1,0:T(4,128)S(1)}, u32[]{:S(2)}, u32[]{:S(2)}) collective-permute-start(f32[4,4,768]{2,1,0:T(4,128)} %norms.1.norm_ref), channel_id=1, source_target_pairs={{0,64},{32,96},{64,0},{96,32},{1,65},{33,97},{65,1},{97,33},{2,66}... | collective-permute-start | bytes 147464 | tf_op jit(solution)/shard_map/ppermute | solution.py:298
  93.7 6.4 %collective-permute-start.3 = (f32[4,4,768]{2,1,0:T(4,128)}, f32[4,4,768]{2,1,0:T(4,128)S(1)}, u32[]{:S(2)}, u32[]{:S(2)}) collective-permute-start(f32[4,4,768]{2,1,0:T(4,128)} %norms.1.norm_ref), channel_id=1, source_target_pairs={{0,96},{32,0},{64,32},{96,64},{1,97},{33,1},{65,33},{97,65},{2,98}... | collective-permute-start | bytes 147464 | tf_op jit(solution)/shard_map/ppermute | solution.py:298
  100.0 0.6 copy-start.3
  100.1 0.6 copy-start.4
  100.1 0.6 copy-start.5
